TPU v7x, 128 devices: a whole 4x4x4 slice. The times are simulated.
128 devices in a mesh: dp: 8 (over x, z_lo), mp: 16 (over z_hi, y, core).
Axes of the slice: x: 4, y: 4, z: 4 (z_hi: 2, z_lo: 2; z = z_hi * 2 + z_lo), core: 2. Of those that a mesh axis runs over, the one named last changes fastest.
Arguments:
- tokens: bfloat16 [16384, 1024], P(('dp', 'mp')), may hold values from -6 to 6
- memory: bfloat16 [16384, 1024], P('dp'), may hold values from -6 to 6
- cotangent: bfloat16 [16384, 1024], P(('dp', 'mp')), may hold values from -6 to 6
- tgt_len: int32 [16], P('dp'), may hold values from 256 to 1024, as said below
- src_len: int32 [16], P('dp'), may hold values from 256 to 1024, as said below
- pair_ids: int32 [16], P('dp'), may hold values from 0 to 63
- loss_weights: int32 [64], replicated, may hold values from 1 to 4
- first_gain: float32 [1024], replicated, may hold values from 0.1 to 1.9
- first_shift: float32 [1024], replicated, may hold values from -1.75 to 1.75
- self_query: bfloat16 [1024, 1024], P(None, 'mp'), may hold values from -0.1875 to 0.1875
- self_query_bias: float32 [1024], P('mp'), may hold values from -3 to 3
- self_key: bfloat16 [1024, 1024], P(None, 'mp'), may hold values from -0.1875 to 0.1875
- self_value: bfloat16 [1024, 1024], P(None, 'mp'), may hold values from -0.1875 to 0.1875
- self_value_bias: float32 [1024], P('mp'), may hold values from -3 to 3
- self_output: bfloat16 [1024, 1024], P('mp'), may hold values from -2.5 to 2.5
- self_output_bias: float32 [1024], replicated, may hold values from -1.75 to 1.75
- second_gain: float32 [1024], replicated, may hold values from 0.1 to 1.9
- second_shift: float32 [1024], replicated, may hold values from -1.75 to 1.75
- cross_query: bfloat16 [1024, 1024], P(None, 'mp'), may hold values from -0.1875 to 0.1875
- cross_query_bias: float32 [1024], P('mp'), may hold values from -3 to 3
- cross_key: bfloat16 [1024, 1024], P(None, 'mp'), may hold values from -0.1875 to 0.1875
- cross_value: bfloat16 [1024, 1024], P(None, 'mp'), may hold values from -0.1875 to 0.1875
- cross_value_bias: float32 [1024], P('mp'), may hold values from -3 to 3
- cross_output: bfloat16 [1024, 1024], P('mp'), may hold values from -2.5 to 2.5
- cross_output_bias: float32 [1024], replicated, may hold values from -1.75 to 1.75
- third_gain: float32 [1024], replicated, may hold values from 0.1 to 1.9
- third_shift: float32 [1024], replicated, may hold values from -1.75 to 1.75
- ffn_in: bfloat16 [1024, 4096], P(None, 'mp'), may hold values from -0.1875 to 0.1875
- ffn_in_bias: float32 [4096], P('mp'), may hold values from -3 to 3
- ffn_out: bfloat16 [4096, 1024], P('mp'), may hold values from -0.125 to 0.125
- ffn_out_bias: float32 [1024], replicated, may hold values from -1.75 to 1.75
Outputs:
- block_out: bfloat16 [16384, 1024], P(('dp', 'mp'))
- tokens_grad: float32 [16384, 1024], P(('dp', 'mp'))
- memory_grad: float32 [16384, 1024], P(('dp', 'mp'))
- first_gain_grad: float32 [1024], replicated
- first_shift_grad: float32 [1024], replicated
- self_query_grad: float32 [1024, 1024], P(None, 'mp')
- self_query_bias_grad: float32 [1024], P('mp')
- self_key_grad: float32 [1024, 1024], P(None, 'mp')
- self_value_grad: float32 [1024, 1024], P(None, 'mp')
- self_value_bias_grad: float32 [1024], P('mp')
- self_output_grad: float32 [1024, 1024], P('mp')
- self_output_bias_grad: float32 [1024], replicated
- second_gain_grad: float32 [1024], replicated
- second_shift_grad: float32 [1024], replicated
- cross_query_grad: float32 [1024, 1024], P(None, 'mp')
- cross_query_bias_grad: float32 [1024], P('mp')
- cross_key_grad: float32 [1024, 1024], P(None, 'mp')
- cross_value_grad: float32 [1024, 1024], P(None, 'mp')
- cross_value_bias_grad: float32 [1024], P('mp')
- cross_output_grad: float32 [1024, 1024], P('mp')
- cross_output_bias_grad: float32 [1024], replicated
- third_gain_grad: float32 [1024], replicated
- third_shift_grad: float32 [1024], replicated
- ffn_in_grad: float32 [1024, 4096], P(None, 'mp')
- ffn_in_bias_grad: float32 [4096], P('mp')
- ffn_out_grad: float32 [4096, 1024], P('mp')
- ffn_out_bias_grad: float32 [1024], replicated
Inputs may be any that keep to these rules, and one draw needn't show every extreme that they name: `tgt_len`: in each group of 2 sequences of one index of dp, one drawn from the seed has exactly 1024 tokens. `src_len`: in each group of 2 sequences of one index of dp, one drawn from the seed has exactly 1024 source tokens.
All inputs are finite; a program needn't handle non-finite values.
Results may differ from a plain program's by a relative error of at most 0.025.
Values may be sent and summed in bfloat16 or wider, within the bound.
No kernel may reach another device: no remote copies, remote signals or barrier semaphores. Data moves between devices by JAX's collectives and lax.ppermute only.
A program may use at most 128 MiB of HBM per device.

v0:
```python
import jax
import jax.numpy as jnp
from jax import lax
from jax.sharding import PartitionSpec as P

HEAD = 64


def matmul(operand, factor):
    return jnp.dot(operand, factor, preferred_element_type=jnp.float32)


def times_transposed(operand, factor):
    return lax.dot_general(
        operand, factor, (((1,), (1,)), ((), ())), preferred_element_type=jnp.float32
    )


def transposed_times(operand, factor):
    return lax.dot_general(
        operand, factor, (((0,), (0,)), ((), ())), preferred_element_type=jnp.float32
    )


def column_sum(inputs):
    return jnp.sum(inputs.astype(jnp.float32), axis=0)


def layer_norm(inputs, norm_gain, norm_shift):
    center = inputs - jnp.mean(inputs, axis=-1, keepdims=True)
    inverse = lax.rsqrt(jnp.mean(center * center, axis=-1, keepdims=True) + 1e-05)
    normal = center * inverse
    return (normal * norm_gain + norm_shift, normal, inverse)


def norm_back(gradient, normal, inverse, norm_gain):
    scaled = gradient * norm_gain
    adjusted = (
        scaled
        - jnp.mean(scaled, axis=-1, keepdims=True)
        - normal * jnp.mean(scaled * normal, axis=-1, keepdims=True)
    )
    return (adjusted * inverse, jnp.sum(gradient * normal, axis=0), jnp.sum(gradient, axis=0))


def score_mask(length, query_len, key_len, causal):
    key_pos = jnp.arange(key_len)
    allowed = (key_pos < length)[None, :]
    if causal:
        allowed = allowed & (key_pos[None, :] <= jnp.arange(query_len)[:, None])
    return allowed[None]


def split_heads(inputs):
    return inputs.reshape(inputs.shape[0], inputs.shape[1] // HEAD, HEAD)


def attend_forward(queries, key_rows, values, length, causal):
    query_len, width = queries.shape
    scores = jnp.einsum(
        "qhe,khe->hqk",
        split_heads(queries),
        split_heads(key_rows),
        preferred_element_type=jnp.float32,
    )
    scores = jnp.where(score_mask(length, query_len, key_rows.shape[0], causal), scores, -1e30)
    highest = jnp.max(scores, axis=-1, keepdims=True)
    raised = jnp.exp(scores - highest)
    totals = jnp.sum(raised, axis=-1, keepdims=True)
    attn_probs = (raised / totals).astype(jnp.bfloat16)
    attn_mixed = jnp.einsum(
        "hqk,khe->qhe", attn_probs, split_heads(values), preferred_element_type=jnp.float32
    )
    return (attn_mixed.reshape(query_len, width), (highest + jnp.log(totals))[..., 0])


def attend_backward(queries, key_rows, values, length, causal, log_total, mixed_grad):
    query_len, width = queries.shape
    key_len = key_rows.shape[0]
    query_heads = split_heads(queries)
    key_heads = split_heads(key_rows)
    grad_heads = split_heads(mixed_grad)
    scores = jnp.einsum("qhe,khe->hqk", query_heads, key_heads, preferred_element_type=jnp.float32)
    allowed = score_mask(length, query_len, key_len, causal)
    attn_probs = jnp.where(allowed, jnp.exp(scores - log_total[..., None]), 0.0)
    value_grad = jnp.einsum(
        "hqk,qhe->khe",
        attn_probs.astype(jnp.bfloat16),
        grad_heads,
        preferred_element_type=jnp.float32,
    )
    prob_grad = jnp.einsum(
        "qhe,khe->hqk", grad_heads, split_heads(values), preferred_element_type=jnp.float32
    )
    inner_sum = jnp.sum(attn_probs * prob_grad, axis=-1, keepdims=True)
    score_grad = (attn_probs * (prob_grad - inner_sum)).astype(jnp.bfloat16)
    query_grad = jnp.einsum(
        "hqk,khe->qhe", score_grad, key_heads, preferred_element_type=jnp.float32
    )
    key_grad = jnp.einsum(
        "hqk,qhe->khe", score_grad, query_heads, preferred_element_type=jnp.float32
    )
    return (
        query_grad.reshape(query_len, width),
        key_grad.reshape(key_len, width),
        value_grad.reshape(key_len, width),
    )


def causal_forward(packed):
    return attend_forward(packed[0], packed[1], packed[2], packed[3], True)


def source_forward(packed):
    return attend_forward(packed[0], packed[1], packed[2], packed[3], False)


def causal_backward(packed):
    return attend_backward(packed[0], packed[1], packed[2], packed[3], True, packed[4], packed[5])


def source_backward(packed):
    return attend_backward(packed[0], packed[1], packed[2], packed[3], False, packed[4], packed[5])


def per_device(
    tokens,
    memory,
    cotangent,
    tgt_len,
    src_len,
    pair_ids,
    loss_weights,
    first_gain,
    first_shift,
    self_query,
    self_query_bias,
    self_key,
    self_value,
    self_value_bias,
    self_output,
    self_output_bias,
    second_gain,
    second_shift,
    cross_query,
    cross_query_bias,
    cross_key,
    cross_value,
    cross_value_bias,
    cross_output,
    cross_output_bias,
    third_gain,
    third_shift,
    ffn_in,
    ffn_in_bias,
    ffn_out,
    ffn_out_bias,
):
    own_rows = tokens.shape[0]
    seq_count = tgt_len.shape[0]
    all_rows = own_rows * lax.axis_size("mp")
    seq_len = all_rows // seq_count
    src_rows = memory.shape[0] // seq_count
    head_scale = HEAD ** (-0.5)
    row_start = lax.axis_index("mp") * own_rows
    whole_tokens = lax.all_gather(tokens, "mp", axis=0, tiled=True).astype(jnp.float32)
    first_norm, first_normal, first_inverse = layer_norm(whole_tokens, first_gain, first_shift)
    first_low = first_norm.astype(jnp.bfloat16)
    queries = (head_scale * (matmul(first_low, self_query) + self_query_bias)).astype(jnp.bfloat16)
    key_rows = matmul(first_low, self_key).astype(jnp.bfloat16)
    values = (matmul(first_low, self_value) + self_value_bias).astype(jnp.bfloat16)
    local_width = queries.shape[1]
    self_packed = (
        queries.reshape(seq_count, seq_len, local_width),
        key_rows.reshape(seq_count, seq_len, local_width),
        values.reshape(seq_count, seq_len, local_width),
        tgt_len,
    )
    self_mixed, self_total = lax.map(causal_forward, self_packed)
    self_mixed = self_mixed.reshape(all_rows, local_width).astype(jnp.bfloat16)
    attended = lax.psum(matmul(self_mixed, self_output), "mp") + self_output_bias
    second_whole = whole_tokens + attended
    second_norm, normal_whole, inverse_whole = layer_norm(second_whole, second_gain, second_shift)
    second_low = second_norm.astype(jnp.bfloat16)
    second_resid = lax.dynamic_slice_in_dim(second_whole, row_start, own_rows, 0)
    second_normal = lax.dynamic_slice_in_dim(normal_whole, row_start, own_rows, 0)
    second_inverse = lax.dynamic_slice_in_dim(inverse_whole, row_start, own_rows, 0)
    cross_queries = (head_scale * (matmul(second_low, cross_query) + cross_query_bias)).astype(
        jnp.bfloat16
    )
    cross_keys = matmul(memory, cross_key).astype(jnp.bfloat16)
    cross_values = (matmul(memory, cross_value) + cross_value_bias).astype(jnp.bfloat16)
    cross_packed = (
        cross_queries.reshape(seq_count, seq_len, local_width),
        cross_keys.reshape(seq_count, src_rows, local_width),
        cross_values.reshape(seq_count, src_rows, local_width),
        src_len,
    )
    cross_mixed, cross_total = lax.map(source_forward, cross_packed)
    cross_mixed = cross_mixed.reshape(all_rows, local_width).astype(jnp.bfloat16)
    third_resid = (
        second_resid
        + lax.psum_scatter(
            matmul(cross_mixed, cross_output).astype(jnp.bfloat16),
            "mp",
            scatter_dimension=0,
            tiled=True,
        ).astype(jnp.float32)
        + cross_output_bias
    )
    third_norm, third_normal, third_inverse = layer_norm(third_resid, third_gain, third_shift)
    third_low = lax.all_gather(third_norm.astype(jnp.bfloat16), "mp", axis=0, tiled=True)
    hidden_pre = matmul(third_low, ffn_in) + ffn_in_bias
    gelu_value, gelu_pull = jax.vjp(
        lambda inputs: jax.nn.gelu(inputs, approximate=True), hidden_pre
    )
    hidden_low = gelu_value.astype(jnp.bfloat16)
    layer_out = (
        third_resid
        + lax.psum_scatter(
            matmul(hidden_low, ffn_out).astype(jnp.bfloat16), "mp", scatter_dimension=0, tiled=True
        ).astype(jnp.float32)
        + ffn_out_bias
    )
    block_out = layer_out.astype(jnp.bfloat16)
    row_ids = row_start + jnp.arange(own_rows)
    positions = row_ids % seq_len
    seq_table = (row_ids // seq_len)[:, None] == jnp.arange(seq_count)[None, :]
    pair_table = pair_ids[:, None] == jnp.arange(loss_weights.shape[0])[None, :]
    seq_weight = 0.5 * jnp.sum(jnp.where(pair_table, loss_weights[None, :], 0), axis=1).astype(
        jnp.float32
    )
    row_weight = jnp.sum(jnp.where(seq_table, seq_weight[None, :], 0.0), axis=1)
    row_length = jnp.sum(jnp.where(seq_table, tgt_len[None, :], 0), axis=1)
    row_weight = jnp.where(positions < row_length, row_weight, 0.0)
    out_grad = cotangent.astype(jnp.float32) * row_weight[:, None]
    out_grad_low = lax.all_gather(out_grad.astype(jnp.bfloat16), "mp", axis=0, tiled=True)
    ffn_out_bias_grad = column_sum(out_grad_low)
    ffn_out_grad = transposed_times(hidden_low, out_grad_low)
    pre_grad = gelu_pull(times_transposed(out_grad_low, ffn_out))[0].astype(jnp.bfloat16)
    ffn_in_bias_grad = column_sum(pre_grad)
    ffn_in_grad = transposed_times(third_low, pre_grad)
    third_back = lax.psum_scatter(
        times_transposed(pre_grad, ffn_in).astype(jnp.bfloat16),
        "mp",
        scatter_dimension=0,
        tiled=True,
    ).astype(jnp.float32)
    third_input, third_gain_part, third_shift_part = norm_back(
        third_back, third_normal, third_inverse, third_gain
    )
    third_grad = out_grad + third_input
    cross_grad_low = lax.all_gather(third_grad.astype(jnp.bfloat16), "mp", axis=0, tiled=True)
    cross_output_bias_grad = column_sum(cross_grad_low)
    cross_output_grad = transposed_times(cross_mixed, cross_grad_low)
    cross_mixed_grad = times_transposed(cross_grad_low, cross_output).astype(jnp.bfloat16)
    cq_grad, ck_grad, cv_grad = lax.map(
        source_backward,
        cross_packed + (cross_total, cross_mixed_grad.reshape(seq_count, seq_len, local_width)),
    )
    cq_grad = cq_grad.reshape(all_rows, local_width).astype(jnp.bfloat16)
    ck_grad = ck_grad.reshape(seq_count * src_rows, local_width).astype(jnp.bfloat16)
    cv_grad = cv_grad.reshape(seq_count * src_rows, local_width).astype(jnp.bfloat16)
    cross_query_grad = head_scale * transposed_times(second_low, cq_grad)
    cross_query_bias_grad = head_scale * column_sum(cq_grad)
    cross_key_grad = transposed_times(memory, ck_grad)
    cross_value_grad = transposed_times(memory, cv_grad)
    cross_value_bias_grad = column_sum(cv_grad)
    second_part = head_scale * times_transposed(cq_grad, cross_query)
    memory_part = times_transposed(ck_grad, cross_key) + times_transposed(cv_grad, cross_value)
    second_back, memory_grad = (
        lax.psum_scatter(
            second_part.astype(jnp.bfloat16), "mp", scatter_dimension=0, tiled=True
        ).astype(jnp.float32),
        lax.psum_scatter(
            memory_part.astype(jnp.bfloat16), "mp", scatter_dimension=0, tiled=True
        ).astype(jnp.float32),
    )
    second_input, second_gain_part, second_shift_part = norm_back(
        second_back, second_normal, second_inverse, second_gain
    )
    second_grad = third_grad + second_input
    self_grad_low = lax.all_gather(second_grad.astype(jnp.bfloat16), "mp", axis=0, tiled=True)
    self_output_bias_grad = column_sum(self_grad_low)
    self_output_grad = transposed_times(self_mixed, self_grad_low)
    self_mixed_grad = times_transposed(self_grad_low, self_output).astype(jnp.bfloat16)
    q_grad, k_grad, v_grad = lax.map(
        causal_backward,
        self_packed + (self_total, self_mixed_grad.reshape(seq_count, seq_len, local_width)),
    )
    q_grad = q_grad.reshape(all_rows, local_width).astype(jnp.bfloat16)
    k_grad = k_grad.reshape(all_rows, local_width).astype(jnp.bfloat16)
    v_grad = v_grad.reshape(all_rows, local_width).astype(jnp.bfloat16)
    self_query_grad = head_scale * transposed_times(first_low, q_grad)
    self_query_bias_grad = head_scale * column_sum(q_grad)
    self_key_grad = transposed_times(first_low, k_grad)
    self_value_grad = transposed_times(first_low, v_grad)
    self_value_bias_grad = column_sum(v_grad)
    first_part = (
        head_scale * times_transposed(q_grad, self_query)
        + times_transposed(k_grad, self_key)
        + times_transposed(v_grad, self_value)
    )
    first_back = lax.psum_scatter(
        first_part.astype(jnp.bfloat16), "mp", scatter_dimension=0, tiled=True
    ).astype(jnp.float32)
    own_normal = lax.dynamic_slice_in_dim(first_normal, row_start, own_rows, 0)
    own_inverse = lax.dynamic_slice_in_dim(first_inverse, row_start, own_rows, 0)
    first_input, first_gain_part, first_shift_part = norm_back(
        first_back, own_normal, own_inverse, first_gain
    )
    tokens_grad = second_grad + first_input
    norm_summed = lax.psum(
        (
            first_gain_part,
            first_shift_part,
            second_gain_part,
            second_shift_part,
            third_gain_part,
            third_shift_part,
        ),
        ("dp", "mp"),
    )
    summed = (
        lax.psum(self_query_grad.astype(jnp.bfloat16), "dp").astype(jnp.float32),
        lax.psum(self_query_bias_grad.astype(jnp.bfloat16), "dp").astype(jnp.float32),
        lax.psum(self_key_grad.astype(jnp.bfloat16), "dp").astype(jnp.float32),
        lax.psum(self_value_grad.astype(jnp.bfloat16), "dp").astype(jnp.float32),
        lax.psum(self_value_bias_grad.astype(jnp.bfloat16), "dp").astype(jnp.float32),
        lax.psum(self_output_grad.astype(jnp.bfloat16), "dp").astype(jnp.float32),
        lax.psum(self_output_bias_grad.astype(jnp.bfloat16), "dp").astype(jnp.float32),
        lax.psum(cross_query_grad.astype(jnp.bfloat16), "dp").astype(jnp.float32),
        lax.psum(cross_query_bias_grad.astype(jnp.bfloat16), "dp").astype(jnp.float32),
        lax.psum(cross_key_grad.astype(jnp.bfloat16), "dp").astype(jnp.float32),
        lax.psum(cross_value_grad.astype(jnp.bfloat16), "dp").astype(jnp.float32),
        lax.psum(cross_value_bias_grad.astype(jnp.bfloat16), "dp").astype(jnp.float32),
        lax.psum(cross_output_grad.astype(jnp.bfloat16), "dp").astype(jnp.float32),
        lax.psum(cross_output_bias_grad.astype(jnp.bfloat16), "dp").astype(jnp.float32),
        lax.psum(ffn_in_grad.astype(jnp.bfloat16), "dp").astype(jnp.float32),
        lax.psum(ffn_in_bias_grad.astype(jnp.bfloat16), "dp").astype(jnp.float32),
        lax.psum(ffn_out_grad.astype(jnp.bfloat16), "dp").astype(jnp.float32),
        lax.psum(ffn_out_bias_grad.astype(jnp.bfloat16), "dp").astype(jnp.float32),
    )
    return (
        block_out,
        tokens_grad,
        memory_grad,
        norm_summed[0],
        norm_summed[1],
        summed[0],
        summed[1],
        summed[2],
        summed[3],
        summed[4],
        summed[5],
        summed[6],
        norm_summed[2],
        norm_summed[3],
        summed[7],
        summed[8],
        summed[9],
        summed[10],
        summed[11],
        summed[12],
        summed[13],
        norm_summed[4],
        norm_summed[5],
        summed[14],
        summed[15],
        summed[16],
        summed[17],
    )


def solution(mesh):
    placed = (
        P(("dp", "mp"), None),
        P("dp", None),
        P(("dp", "mp"), None),
        P("dp"),
        P("dp"),
        P("dp"),
        P(),
        P(),
        P(),
        P(None, "mp"),
        P("mp"),
        P(None, "mp"),
        P(None, "mp"),
        P("mp"),
        P("mp", None),
        P(),
        P(),
        P(),
        P(None, "mp"),
        P("mp"),
        P(None, "mp"),
        P(None, "mp"),
        P("mp"),
        P("mp", None),
        P(),
        P(),
        P(),
        P(None, "mp"),
        P("mp"),
        P("mp", None),
        P(),
    )
    return jax.shard_map(
        per_device,
        mesh=mesh,
        in_specs=placed,
        out_specs=(
            P(("dp", "mp"), None),
            P(("dp", "mp"), None),
            P(("dp", "mp"), None),
            P(),
            P(),
            P(None, "mp"),
            P("mp"),
            P(None, "mp"),
            P(None, "mp"),
            P("mp"),
            P("mp", None),
            P(),
            P(),
            P(),
            P(None, "mp"),
            P("mp"),
            P(None, "mp"),
            P(None, "mp"),
            P("mp"),
            P("mp", None),
            P(),
            P(),
            P(),
            P(None, "mp"),
            P("mp"),
            P("mp", None),
            P(),
        ),
        check_vma=False,
    )
```

profile of v0, /device:TPU:0, one launch (start us, length us, event | category | flops | bytes accessed | tf_op | source)
XLA Modules:
  0.0 1236.9 jit_solution(13756909200319876928)
XLA Ops:
  8.0 61.1 %all-gather.6.cloned.1.call-done = bf16[2048,1024]{1,0:T(8,128)(2,1)} async-done(((bf16[128,1024]{1,0:T(8,128)(2,1)}), bf16[2048,1024]{1,0:T(8,128)(2,1)}) %all-gather.6.cloned.1.call-update) | async-done | bytes 4194320 | tf_op jit(solution)/shard_map/all_gather | solution.py:166
  69.1 3.0 convert_reduce_fusion
  74.0 4.1 fusion.96
  81.7 3.6 fusion.102
  85.6 3.6 fusion.101
  89.6 7.1 while.52
  97.5 4.5 fusion.150
  102.9 3.6 fusion.103
  106.8 3.6 convolution_convert_fusion.5
  110.7 154.1 %all-reduce.6.cloned.1.call-done = f32[2048,1024]{1,0:T(8,128)} async-done(((f32[2048,1024]{1,0:T(8,128)}), f32[2048,1024]{1,0:T(8,128)}) %all-reduce.6.cloned.1.call-update) | async-done | bytes 8388624 | tf_op jit(solution)/shard_map/psum | solution.py:181
  264.8 5.7 fusion.149
  274.7 3.2 copy-done.5
  279.6 7.9 while.53
  287.7 3.3 convolution_convert_fusion.2
  292.4 79.5 %reduce-scatter.7.cloned.1.call-done = bf16[128,1024]{1,0:T(8,128)(2,1)} async-done(((bf16[2048,1024]{1,0:T(8,128)(2,1)}), bf16[128,1024]{1,0:T(8,128)(2,1)}) %reduce-scatter.7.cloned.1.call-update) | async-done | bytes 262160 | tf_op jit(solution)/shard_map/reduce_scatter | solution.py:203
  374.6 55.1 %all-gather.10.cloned.1.call-done = bf16[2048,1024]{1,0:T(8,128)(2,1)} async-done(((bf16[128,1024]{1,0:T(8,128)(2,1)}), bf16[2048,1024]{1,0:T(8,128)(2,1)}) %all-gather.10.cloned.1.call-update) | async-done | bytes 4194320 | tf_op jit(solution)/shard_map/all_gather | solution.py:237
  429.6 4.9 fusion.151
  434.5 53.0 %all-gather.8.cloned.1.call-done = bf16[2048,1024]{1,0:T(8,128)(2,1)} async-done(((bf16[128,1024]{1,0:T(8,128)(2,1)}), bf16[2048,1024]{1,0:T(8,128)(2,1)}) %all-gather.8.cloned.1.call-update) | async-done | bytes 4194320 | tf_op jit(solution)/shard_map/all_gather | solution.py:212
  487.5 7.1 fusion.142
  495.6 3.2 convolution_convert_fusion
  499.9 5.0 convolution_convert_fusion.1
  505.0 73.2 %reduce-scatter.11.cloned.1.call-done = bf16[128,1024]{1,0:T(8,128)(2,1)} async-done(((bf16[2048,1024]{1,0:T(8,128)(2,1)}), bf16[128,1024]{1,0:T(8,128)(2,1)}) %reduce-scatter.11.cloned.1.call-update) | async-done | bytes 262160 | tf_op jit(solution)/shard_map/reduce_scatter | solution.py:243
  579.9 81.2 %reduce-scatter.9.cloned.1.call-done = bf16[128,1024]{1,0:T(8,128)(2,1)} async-done(((bf16[2048,1024]{1,0:T(8,128)(2,1)}), bf16[128,1024]{1,0:T(8,128)(2,1)}) %reduce-scatter.9.cloned.1.call-update) | async-done | bytes 262160 | tf_op jit(solution)/shard_map/reduce_scatter | solution.py:220
  661.1 2.3 fusion.146
  663.7 55.2 %all-gather.12.cloned.1.call-done = bf16[2048,1024]{1,0:T(8,128)(2,1)} async-done(((bf16[128,1024]{1,0:T(8,128)(2,1)}), bf16[2048,1024]{1,0:T(8,128)(2,1)}) %all-gather.12.cloned.1.call-update) | async-done | bytes 4194320 | tf_op jit(solution)/shard_map/all_gather | solution.py:253
  719.0 3.6 convolution_convert_fusion.4
  722.9 13.3 %while.54 = (s32[]{:T(128)}, bf16[2,1024,64]{1,2,0:T(8,128)(2,1)S(1)}, bf16[2,1024,64]{1,2,0:T(8,128)(2,1)S(1)}, bf16[2,1024,64]{1,2,0:T(8,128)(2,1)S(1)}, bf16[...) while((s32[]{:T(128)}, ...), condition=%wide.region_25.26_spmd, body=%wide.region_23.25_spmd.sunk | while | flops 683671552 | bytes 34116744 | solution.py:257
  736.9 3.2 multiply_convert_fusion.2
  741.1 78.4 %reduce-scatter.13.cloned.1.call-done = bf16[128,1024]{1,0:T(8,128)(2,1)} async-done(((bf16[2048,1024]{1,0:T(8,128)(2,1)}), bf16[128,1024]{1,0:T(8,128)(2,1)}) %reduce-scatter.13.cloned.1.call-update) | async-done | bytes 262160 | tf_op jit(solution)/shard_map/reduce_scatter | solution.py:272
  820.8 2.2 fusion.144
  823.6 4.4 convolution_convert_fusion.8
  828.0 2.3 convolution_convert_fusion.7
  837.4 3.3 add_convert_fusion
  840.9 3.7 convolution_convert_fusion.11
  844.7 33.0 %all-gather.14.cloned.1.call-done = bf16[2048,1024]{1,0:T(8,128)(2,1)} async-done(((bf16[128,1024]{1,0:T(8,128)(2,1)}), bf16[2048,1024]{1,0:T(8,128)(2,1)}) %all-gather.14.cloned.1.call-update) | async-done | bytes 4194320 | tf_op jit(solution)/shard_map/all_gather | solution.py:283
  877.7 3.6 convolution_convert_fusion.3
  881.7 12.8 %while.55 = (s32[]{:T(128)}, bf16[2,1024,64]{1,2,0:T(8,128)(2,1)S(1)}, bf16[2,1024,64]{1,2,0:T(8,128)(2,1)S(1)}, bf16[2,1024,64]{1,2,0:T(8,128)(2,1)S(1)}, bf16[...) while((s32[]{:T(128)}, ...), condition=%wide.region_31.32_spmd, body=%wide.region_29.31_spmd.sunk | while | flops 681574400 | bytes 34106504 | solution.py:287
  894.6 4.1 convolution_convert_fusion.10
  906.1 3.2 add_convert_fusion.1
  910.1 2.9 reduce_sum.343
  913.0 3.1 reduce_sum.339
  916.4 44.5 %reduce-scatter.17.cloned.1.call-done = bf16[128,1024]{1,0:T(8,128)(2,1)} async-done(((bf16[2048,1024]{1,0:T(8,128)(2,1)}), bf16[128,1024]{1,0:T(8,128)(2,1)}) %reduce-scatter.17.cloned.1.call-update) | async-done | bytes 262160 | tf_op jit(solution)/shard_map/reduce_scatter | solution.py:275
  962.7 2.9 reduce_sum.334
  965.9 19.5 %all-reduce.1 = (bf16[64]{0:T(256)(128)(2,1)S(1)}, bf16[64]{0:T(256)(128)(2,1)S(1)}, bf16[1024]{0:T(1024)(128)(2,1)S(1)}, bf16[64]{0:T(256)(128)(2,1)S(1)}, bf16...) all-reduce(bf16[64]{0:T(256)(128)(2,1)S(1)} %multiply_convert_fusio, ...), channel_id=1, replica_groups=mesh['dp'=8,'mp'=16] {'dp'}, use_global_device_ids=true, to_apply=%region_42.43 | all-reduce | flops 3584 | bytes 14336 | tf_op jit(solution)/shard_map/psum | solution.py:326
  989.9 86.0 %all-reduce.8.cloned.1.call-done = (bf16[1024,64]{0,1:T(8,128)(2,1)}, bf16[1024,64]{0,1:T(8,128)(2,1)}, bf16[1024,64]{0,1:T(8,128)(2,1)}, bf16[64,1024]{1,0:T(8,...) async-done(((bf16[1024,64]{0,1:T(8,128)(2,1)}, ...) | async-done | bytes 2097168 | tf_op jit(solution)/shard_map/psum | solution.py:325
  1089.0 2.1 convert_element_type.369
  1092.2 69.5 %reduce-scatter.15.cloned.1.call-done = bf16[128,1024]{1,0:T(8,128)(2,1)} async-done(((bf16[2048,1024]{1,0:T(8,128)(2,1)}), bf16[128,1024]{1,0:T(8,128)(2,1)}) %reduce-scatter.15.cloned.1.call-update) | async-done | bytes 262160 | tf_op jit(solution)/shard_map/reduce_scatter | solution.py:304
  1163.1 65.0 %all-reduce = (f32[1024]{0:T(1024)}, f32[1024]{0:T(1024)}, f32[1024]{0:T(1024)}, f32[1024]{0:T(1024)}, f32[1024]{0:T(1024)}, /*index=5*/f32[1024]{0:T(1024)}) all-reduce(f32[1024]{0:T(1024)S(1)} %get-tuple-element.325, f32[1024]{0:T(1024)S(1)} %get-tuple-element.334, ...), channel_id=1, replica_groups=mesh['dp'=8,'mp'=16] {'dp','mp'}, use_global_device_ids=true, to_apply=%region_37.38 | all-reduce | flops 6144 | bytes 49152 | tf_op jit(solution)/shard_map/psum | solution.py:313
  (325 shorter events, 108.0 us)
Async XLA Ops:
  7.2 480.3 %copy-start = (bf16[1024,256]{1,0:T(8,128)(2,1)S(1)}, bf16[1024,256]{1,0:T(8,128)(2,1)}, u32[]{:S(2)}) copy-start(bf16[1024,256]{1,0:T(8,128)(2,1)} %param.66) | copy-start | bytes 1572868
  7.2 61.9 %all-gather.6.cloned.1.call-start = ((), (), s32[]{:S(2)}) async-start(), calls=%async_computation.6 | async-start | bytes 4456448 | tf_op jit(solution)/shard_map/all_gather | solution.py:166
  8.0 256.8 %all-reduce.6.cloned.1.call-start = ((), (), s32[]{:S(2)}) async-start(), calls=%async_computation.7 | async-start | bytes 16777216 | tf_op jit(solution)/shard_map/psum | solution.py:181
  8.0 66.0 %copy-start.44 = (f32[1024]{0:T(1024)S(1)}, f32[1024]{0:T(1024)}, u32[]{:S(2)}) copy-start(f32[1024]{0:T(1024)} %param.46) | copy-start | bytes 12292
  8.0 65.9 %copy-start.51 = (f32[1024]{0:T(1024)S(1)}, f32[1024]{0:T(1024)}, u32[]{:S(2)}) copy-start(f32[1024]{0:T(1024)} %param.47) | copy-start | bytes 12292
  74.0 6.0 copy-start.34
  89.5 8.0 copy-start.30
  96.7 5.4 copy-start.9
  96.7 5.4 copy-start.11
  96.7 5.4 copy-start.13
  96.7 5.6 copy-start.40
  102.1 4.7 copy-start.26
  102.1 269.8 %reduce-scatter.7.cloned.1.call-start = ((), (), s32[]{:S(2)}) async-start(), calls=%async_computation.8 | async-start | bytes 4456448 | tf_op jit(solution)/shard_map/reduce_scatter | solution.py:203
  106.5 158.2 %copy-start.55 = (f32[1024]{0:T(1024)S(1)}, f32[1024]{0:T(1024)}, u32[]{:S(2)}) copy-start(f32[1024]{0:T(1024)} %param.54) | copy-start | bytes 12292
  279.6 8.0 copy-start.39
  287.7 84.2 %copy-start.52 = (f32[1024]{0:T(1024)S(1)}, f32[1024]{0:T(1024)}, u32[]{:S(2)}) copy-start(f32[1024]{0:T(1024)} %param.63) | copy-start | bytes 12292
  291.0 82.4 %copy-start.43 = (f32[1024]{0:T(1024)S(1)}, f32[1024]{0:T(1024)}, u32[]{:S(2)}) copy-start(f32[1024]{0:T(1024)} %param.64) | copy-start | bytes 12292
  291.0 82.4 %copy-start.53 = (f32[1024]{0:T(1024)S(1)}, f32[1024]{0:T(1024)}, u32[]{:S(2)}) copy-start(f32[1024]{0:T(1024)} %param.65) | copy-start | bytes 12292
  291.0 138.6 %all-gather.10.cloned.1.call-start = ((), (), s32[]{:S(2)}) async-start(), calls=%async_computation.11 | async-start | bytes 4456448 | tf_op jit(solution)/shard_map/all_gather | solution.py:237
  292.3 195.2 %all-gather.8.cloned.1.call-start = ((), (), s32[]{:S(2)}) async-start(), calls=%async_computation.9 | async-start | bytes 4456448 | tf_op jit(solution)/shard_map/all_gather | solution.py:212
  374.3 113.3 %copy-start.62 = (f32[256]{0:T(256)S(1)}, f32[256]{0:T(256)}, u32[]{:S(2)}) copy-start(f32[256]{0:T(256)} %param.67) | copy-start | bytes 3076
  374.3 203.8 %reduce-scatter.11.cloned.1.call-start = ((), (), s32[]{:S(2)}) async-start(), calls=%async_computation.12 | async-start | bytes 4456448 | tf_op jit(solution)/shard_map/reduce_scatter | solution.py:243
  498.9 162.2 %reduce-scatter.9.cloned.1.call-start = ((), (), s32[]{:S(2)}) async-start(), calls=%async_computation.10 | async-start | bytes 4456448 | tf_op jit(solution)/shard_map/reduce_scatter | solution.py:220
  504.9 156.2 %copy-start.54 = (f32[1024]{0:T(1024)S(1)}, f32[1024]{0:T(1024)}, u32[]{:S(2)}) copy-start(f32[1024]{0:T(1024)} %param.69) | copy-start | bytes 12292
  504.9 214.0 %all-gather.12.cloned.1.call-start = ((), (), s32[]{:S(2)}) async-start(), calls=%async_computation.13 | async-start | bytes 4456448 | tf_op jit(solution)/shard_map/all_gather | solution.py:253
  663.4 59.5 %copy-start.66 = (s32[2]{0:T(128)S(1)}, s32[2]{0:T(128)}, u32[]{:S(2)}) copy-start(s32[2]{0:T(128)} %param.43) | copy-start | bytes 28
  663.4 156.0 %reduce-scatter.13.cloned.1.call-start = ((), (), s32[]{:S(2)}) async-start(), calls=%async_computation.14 | async-start | bytes 4456448 | tf_op jit(solution)/shard_map/reduce_scatter | solution.py:272
  736.9 83.9 %copy-start.21 = (f32[128,1024]{1,0:T(8,128)S(1)}, f32[128,1024]{1,0:T(8,128)}, u32[]{:S(2)}) copy-start(f32[128,1024]{1,0:T(8,128)} %get-tuple-element.432) | copy-start | bytes 1572868
  740.2 83.4 %copy-start.19 = (bf16[2048,256]{1,0:T(8,128)(2,1)S(1)}, bf16[2048,256]{1,0:T(8,128)(2,1)}, u32[]{:S(2)}) copy-start(bf16[2048,256]{1,0:T(8,128)(2,1)} %copy-done.18) | copy-start | bytes 3145732
  740.2 137.5 %all-gather.14.cloned.1.call-start = ((), (), s32[]{:S(2)}) async-start(), calls=%async_computation.15 | async-start | bytes 4456448 | tf_op jit(solution)/shard_map/all_gather | solution.py:283
  823.0 137.9 %reduce-scatter.17.cloned.1.call-start = ((), (), s32[]{:S(2)}) async-start(), calls=%async_computation.17 | async-start | bytes 4456448 | tf_op jit(solution)/shard_map/reduce_scatter | solution.py:275
  823.5 4.5 copy-start.15
  823.5 4.5 copy-start.69
  840.7 37.0 %copy-start.31 = (bf16[64,1024]{1,0:T(8,128)(2,1)S(1)}, bf16[64,1024]{1,0:T(8,128)(2,1)}, u32[]{:S(2)}) copy-start(bf16[64,1024]{1,0:T(8,128)(2,1)} %param.53) | copy-start | bytes 393220
  840.7 235.1 %all-reduce.8.cloned.1.call-start = ((), (), s32[]{:S(2)}) async-start(), calls=%async_computation.18 | async-start | bytes 4194304 | tf_op jit(solution)/shard_map/psum | solution.py:325
  844.6 37.0 %copy-start.10 = (bf16[2,1024,64]{2,1,0:T(8,128)(2,1)S(1)}, bf16[2,1024,64]{2,1,0:T(8,128)(2,1)}, u32[]{:S(2)}) copy-start(bf16[2,1024,64]{2,1,0:T(8,128)(2,1)} %copy-done.9) | copy-start | bytes 786436
  844.6 37.0 %copy-start.12 = (bf16[2,1024,64]{2,1,0:T(8,128)(2,1)S(1)}, bf16[2,1024,64]{2,1,0:T(8,128)(2,1)}, u32[]{:S(2)}) copy-start(bf16[2,1024,64]{2,1,0:T(8,128)(2,1)} %copy-done.11) | copy-start | bytes 786436
  844.6 37.0 %copy-start.14 = (bf16[2,1024,64]{2,1,0:T(8,128)(2,1)S(1)}, bf16[2,1024,64]{2,1,0:T(8,128)(2,1)}, u32[]{:S(2)}) copy-start(bf16[2,1024,64]{2,1,0:T(8,128)(2,1)} %copy-done.13) | copy-start | bytes 786436
  844.6 37.0 %copy-start.41 = (f32[2,1,1024]{2,1,0:T(1,128)S(1)}, f32[2,1,1024]{2,1,0:T(1,128)}, u32[]{:S(2)}) copy-start(f32[2,1,1024]{2,1,0:T(1,128)} %copy-done.40) | copy-start | bytes 24580
  844.6 37.1 %copy-start.68 = (s32[2]{0:T(128)S(1)}, s32[2]{0:T(128)}, u32[]{:S(2)}) copy-start(s32[2]{0:T(128)} %param.42) | copy-start | bytes 28
  903.3 258.4 %reduce-scatter.15.cloned.1.call-start = ((), (), s32[]{:S(2)}) async-start(), calls=%async_computation.16 | async-start | bytes 4456448 | tf_op jit(solution)/shard_map/reduce_scatter | solution.py:304
  913.0 52.9 %copy-start.60 = (bf16[256]{0:T(256)(128)(2,1)S(1)}, bf16[256]{0:T(256)(128)(2,1)}, u32[]{:S(2)}) copy-start(bf16[256]{0:T(256)(128)(2,1)} %get-tuple-element.427) | copy-start | bytes 1540
  965.6 196.1 %copy-start.45 = (f32[1024]{0:T(1024)S(1)}, f32[1024]{0:T(1024)}, u32[]{:S(2)}) copy-start(f32[1024]{0:T(1024)} %param.46) | copy-start | bytes 12292
  965.6 197.4 %copy-start.49 = (f32[1024]{0:T(1024)S(1)}, f32[1024]{0:T(1024)}, u32[]{:S(2)}) copy-start(f32[1024]{0:T(1024)} %get-tuple-element.327) | copy-start | bytes 12292
  965.6 197.4 %copy-start.50 = (f32[1024]{0:T(1024)S(1)}, f32[1024]{0:T(1024)}, u32[]{:S(2)}) copy-start(f32[1024]{0:T(1024)} %get-tuple-element.332) | copy-start | bytes 12292
  965.6 262.4 %copy-start.20 = (f32[128,1024]{1,0:T(8,128)S(1)}, f32[128,1024]{1,0:T(8,128)}, u32[]{:S(2)}) copy-start(f32[128,1024]{1,0:T(8,128)} %get-tuple-element.430) | copy-start | bytes 1572868
  1075.8 15.2 %copy-start.38 = (bf16[256,1024]{1,0:T(8,128)(2,1)S(1)}, bf16[256,1024]{1,0:T(8,128)(2,1)}, u32[]{:S(2)}) copy-start(bf16[256,1024]{1,0:T(8,128)(2,1)} %get-tuple-element.426) | copy-start | bytes 1572868
  1077.5 152.6 %copy-start.1 = (bf16[1024,256]{1,0:T(8,128)(2,1)S(1)}, bf16[1024,256]{1,0:T(8,128)(2,1)}, u32[]{:S(2)}) copy-start(bf16[1024,256]{1,0:T(8,128)(2,1)} %param.66) | copy-start | bytes 1572868
  (37 other events, 100.7 us)
Sparse Core Ops, SparseCore 0:
  10.5 58.5 all-gather.5
  102.2 162.5 all-reduce.5
  291.2 80.6 reduce-scatter.6
  375.1 54.5 all-gather.9
  432.8 54.7 all-gather.7
  499.0 79.0 reduce-scatter.10
  582.2 78.8 reduce-scatter.8
  664.4 54.5 all-gather.11
  740.3 79.0 reduce-scatter.12
  823.1 54.5 all-gather.13
  881.8 79.1 reduce-scatter.16
  966.8 108.9 all-reduce.7
  1080.4 81.1 reduce-scatter.14
where the time goes:
time: 1250 us; the launch traced here: 1240 us
  waiting for transfers between devices  925 us (74%)
  matrix products  112 us (9%)
  blocking collectives  84.5 us (7%)
  other arithmetic  76 us (6%)
  local copies, waits for them, and re-layouts  22 us (2%)
  between operations  15.1 us (1%)
    psum x1, waiting for transfers between devices, per_device(): lax.psum(matmul(self_mixed, self_output), 'mp') + self_output_bias  154 us
    psum x1, waiting for transfers between devices, per_device(): lax.psum(self_query_grad.astype(jnp.bfloat16), 'dp').astype(jnp.float32)  86 us
    reduce_scatter x1, waiting for transfers between devices, per_device(): lax.psum_scatter(matmul(hidden_low, ffn_out).astype(jnp.bfloat16), 'mp',...  81.2 us
    reduce_scatter x1, waiting for transfers between devices, per_device(): lax.psum_scatter(matmul(cross_mixed, cross_output).astype(jnp.bfloat16),...  79.5 us
    reduce_scatter x1, waiting for transfers between devices, per_device(): lax.psum_scatter(second_part.astype(jnp.bfloat16), 'mp', scatter_dimensio...  78.4 us
    reduce_scatter x1, waiting for transfers between devices, per_device(): lax.psum_scatter(times_transposed(pre_grad, ffn_in).astype(jnp.bfloat16),...  73.2 us
    reduce_scatter x1, waiting for transfers between devices, per_device(): lax.psum_scatter(first_part.astype(jnp.bfloat16), 'mp', scatter_dimension...  69.5 us
    psum x1, blocking collectives, per_device(): lax.psum((first_gain_part, first_shift_part, second_gain_part, second_shi...  65 us
  transfers between devices with their start and end apart: 13, of which 13 were waited for; matrix products, arithmetic and copies ran while one was open for 9% of the time, Pallas kernels for 0%

commit v1 on v0

v1 whole, which is shorter than its diff:
```python
import jax
import jax.numpy as jnp
from jax import lax
from jax.sharding import Mesh, PartitionSpec as P

HEAD = 64
BF = jnp.bfloat16
F32 = jnp.float32


def nn(a, b):
    return jnp.dot(a, b, preferred_element_type=F32)


def nt(a, b):
    return lax.dot_general(a, b, (((1,), (1,)), ((), ())), preferred_element_type=F32)


def tn(a, b):
    return lax.dot_general(a, b, (((0,), (0,)), ((), ())), preferred_element_type=F32)


def ring(n, k):
    return [(i, (i + k) % n) for i in range(n)]


def from_core(v):
    return lax.ppermute(v, "c", ring(2, 1))


def from_half(v):
    return lax.ppermute(v, ("zl", "zh"), [(i, 3 - i) for i in range(4)])


def from_zl(v):
    return lax.ppermute(v, "zl", ring(2, 1))


def sibling_heads(v):
    return jnp.concatenate([v[:, 128:256], v[:, :128], v[:, 384:], v[:, 256:384]], axis=1)


def gather_rel(v, axis="y"):
    return [v] + [lax.ppermute(v, axis, ring(4, 4 - r)) for r in range(1, 4)]


def gather_rows(v):
    return jnp.concatenate(gather_rel(v), axis=0)


def scatter_sum(blocks, axis="y"):
    got = [lax.ppermute(blocks[r], axis, ring(4, r)) for r in range(1, 4)]
    total = blocks[0].astype(F32)
    for g in got:
        total = total + g.astype(F32)
    return total


def scatter_rows(part):
    part = part.astype(BF)
    return scatter_sum([part[r * 128 : (r + 1) * 128] for r in range(4)])


def whole_sum(vectors):
    n = vectors.shape[0]

    def spread(v, axes, count):
        return jnp.sum(lax.all_to_all(jnp.broadcast_to(v[None], (count,) + v.shape), axes, 0, 0), axis=0)

    v = spread(vectors, ("zh", "y", "c"), 16)
    return spread(v, ("x", "zl"), 8)


def pick(index, blocks):
    out = blocks[0]
    for i in range(1, len(blocks)):
        out = jnp.where(index == i, blocks[i], out)
    return out


def grad_sum(parts):
    rows = parts.shape[0] // 4
    low = parts.astype(BF)
    mine = parts[: 2 * rows] + from_core(low[2 * rows :]).astype(F32)
    set_sum = mine[:rows] + from_half(mine[rows:].astype(BF)).astype(F32)
    set_low = set_sum.astype(BF)
    zl = lax.axis_index("zl")
    x = lax.axis_index("x")
    half = rows // 2
    keep = lax.dynamic_slice_in_dim(set_sum, zl * half, half, 0)
    send = lax.dynamic_slice_in_dim(set_low, (1 - zl) * half, half, 0)
    halves = (keep + from_zl(send).astype(F32)).astype(BF)
    quarter = half // 4
    blocks = [lax.dynamic_slice_in_dim(halves, ((x + r) % 4) * quarter, quarter, 0) for r in range(4)]
    piece = scatter_sum(blocks, "x").astype(BF)
    got = gather_rel(piece, "x")
    whole = jnp.zeros((half, parts.shape[1]), BF)
    for r in range(4):
        whole = lax.dynamic_update_slice_in_dim(whole, got[r], ((x + r) % 4) * quarter, 0)
    other = from_zl(whole)
    low_half = jnp.where(zl == 0, whole, other)
    high_half = jnp.where(zl == 0, other, whole)
    return jnp.concatenate([low_half, high_half], axis=0).astype(F32)


def layer_norm(inputs, gain, shift):
    center = inputs - jnp.mean(inputs, axis=-1, keepdims=True)
    inverse = lax.rsqrt(jnp.mean(center * center, axis=-1, keepdims=True) + 1e-05)
    normal = center * inverse
    return normal * gain + shift, normal, inverse


def norm_back(gradient, normal, inverse, gain):
    scaled = gradient * gain
    adjusted = (
        scaled
        - jnp.mean(scaled, axis=-1, keepdims=True)
        - normal * jnp.mean(scaled * normal, axis=-1, keepdims=True)
    )
    return adjusted * inverse, jnp.sum(gradient * normal, axis=0), jnp.sum(gradient, axis=0)


def split_heads(v):
    return v.reshape(v.shape[0], v.shape[1] // HEAD, HEAD)


def attend_forward(queries, keys, values, allowed):
    scores = jnp.einsum("qhe,khe->hqk", split_heads(queries), split_heads(keys), preferred_element_type=F32)
    scores = jnp.where(allowed[None], scores, -1e30)
    highest = jnp.max(scores, axis=-1, keepdims=True)
    raised = jnp.exp(scores - highest)
    totals = jnp.sum(raised, axis=-1, keepdims=True)
    probs = (raised / totals).astype(BF)
    mixed = jnp.einsum("hqk,khe->qhe", probs, split_heads(values), preferred_element_type=F32)
    return mixed.reshape(queries.shape), (highest + jnp.log(totals))[..., 0]


def attend_backward(queries, keys, values, allowed, log_total, mixed_grad):
    qh, kh, gh = split_heads(queries), split_heads(keys), split_heads(mixed_grad)
    scores = jnp.einsum("qhe,khe->hqk", qh, kh, preferred_element_type=F32)
    probs = jnp.where(allowed[None], jnp.exp(scores - log_total[..., None]), 0.0)
    value_grad = jnp.einsum("hqk,qhe->khe", probs.astype(BF), gh, preferred_element_type=F32)
    prob_grad = jnp.einsum("qhe,khe->hqk", gh, split_heads(values), preferred_element_type=F32)
    inner = jnp.sum(probs * prob_grad, axis=-1, keepdims=True)
    score_grad = (probs * (prob_grad - inner)).astype(BF)
    query_grad = jnp.einsum("hqk,khe->qhe", score_grad, kh, preferred_element_type=F32)
    key_grad = jnp.einsum("hqk,qhe->khe", score_grad, qh, preferred_element_type=F32)
    return (
        query_grad.reshape(queries.shape),
        key_grad.reshape(keys.shape),
        value_grad.reshape(keys.shape),
    )


def per_device(
    tokens,
    memory,
    cotangent,
    tgt_len,
    src_len,
    pair_ids,
    loss_weights,
    first_gain,
    first_shift,
    self_query,
    self_query_bias,
    self_key,
    self_value,
    self_value_bias,
    self_output,
    self_output_bias,
    second_gain,
    second_shift,
    cross_query,
    cross_query_bias,
    cross_key,
    cross_value,
    cross_value_bias,
    cross_output,
    cross_output_bias,
    third_gain,
    third_shift,
    ffn_in,
    ffn_in_bias,
    ffn_out,
    ffn_out_bias,
):
    zh = lax.axis_index("zh")
    y = lax.axis_index("y")
    c = lax.axis_index("c")
    scale = HEAD ** (-0.5)

    def sets(v):
        pair = jnp.concatenate([v, from_half(v)], axis=0)
        return jnp.concatenate([pair, from_core(pair)], axis=0)

    def heads_of(packed, count, index):
        return jnp.concatenate(
            [packed[(s * count + index) * 64 : (s * count + index + 1) * 64] for s in range(4)], axis=0
        )

    tok = tokens.astype(F32)
    first_norm, first_normal, first_inverse = layer_norm(tok, first_gain, first_shift)
    first = gather_rows(first_norm.astype(BF))

    pack_one = sets(jnp.concatenate([self_query.T, self_key.T, self_value.T], axis=0))
    wq, wk, wv = (heads_of(pack_one, 3, i) for i in range(3))
    bias_row = jnp.concatenate(
        [self_query_bias, self_value_bias, cross_query_bias, cross_value_bias, ffn_in_bias]
    ).reshape(1, 512)
    biases = sets(bias_row)
    bq, bv, cbq, cbv = (biases[:, i * 64 : (i + 1) * 64].reshape(256) for i in range(4))
    fb = biases[:, 256:].reshape(1024)
    pack_two = sets(
        jnp.concatenate([self_output, cross_query.T, cross_key.T, cross_value.T, cross_output], axis=0)
    )
    wo, cwq, cwk, cwv, cwo = (heads_of(pack_two, 5, i) for i in range(5))
    win = sets(ffn_in.T)
    wout = sets(ffn_out)

    tl = lax.dynamic_index_in_dim(tgt_len, zh, 0, False)
    sl = lax.dynamic_index_in_dim(src_len, zh, 0, False)
    pair = lax.dynamic_index_in_dim(pair_ids, zh, 0, False)
    weight = 0.5 * lax.dynamic_index_in_dim(loss_weights, pair, 0, False).astype(F32)
    own_pos = (2 * y + c) * 128 + jnp.arange(128)
    out_grad = cotangent.astype(F32) * jnp.where(own_pos < tl, weight, 0.0)[:, None]
    out_grad_low = out_grad.astype(BF)
    og = gather_rows(out_grad_low)

    queries = (scale * (nt(first, wq) + bq)).astype(BF)
    keys = nt(first, wk).astype(BF)
    values = (nt(first, wv) + bv).astype(BF)
    kv = jnp.concatenate([keys, values], axis=1)
    kv = jnp.concatenate([kv, sibling_heads(from_core(kv))], axis=0)
    all_keys, all_values = kv[:, :256], kv[:, 256:]
    block = (2 * ((y + jnp.arange(4)) % 4))[:, None] * 128 + jnp.arange(128)[None, :]
    q_pos = (block + c * 128).reshape(512)
    k_pos = jnp.concatenate([q_pos, (block + (1 - c) * 128).reshape(512)])
    causal = (k_pos[None, :] <= q_pos[:, None]) & (k_pos < tl)[None, :]
    self_mixed, self_total = attend_forward(queries, all_keys, all_values, causal)
    self_mixed = self_mixed.astype(BF)
    second_resid = tok + scatter_rows(nn(self_mixed, wo)) + self_output_bias
    second_norm, second_normal, second_inverse = layer_norm(second_resid, second_gain, second_shift)
    second = gather_rows(second_norm.astype(BF))

    mem = lax.dynamic_slice_in_dim(memory, zh * 1024, 1024, 0)
    cross_queries = (scale * (nt(second, cwq) + cbq)).astype(BF)
    cross_keys = nt(mem, cwk).astype(BF)
    cross_values = (nt(mem, cwv) + cbv).astype(BF)
    source = jnp.broadcast_to((jnp.arange(1024) < sl)[None, :], (512, 1024))
    cross_mixed, cross_total = attend_forward(cross_queries, cross_keys, cross_values, source)
    cross_mixed = cross_mixed.astype(BF)
    third_resid = second_resid + scatter_rows(nn(cross_mixed, cwo)) + cross_output_bias
    third_norm, third_normal, third_inverse = layer_norm(third_resid, third_gain, third_shift)
    third = gather_rows(third_norm.astype(BF))

    hidden_pre = nt(third, win) + fb
    gelu_value, gelu_pull = jax.vjp(lambda v: jax.nn.gelu(v, approximate=True), hidden_pre)
    hidden = gelu_value.astype(BF)
    pre_grad = gelu_pull(nt(og, wout))[0].astype(BF)
    third_back = scatter_rows(nn(pre_grad, win))
    layer_out = third_resid + scatter_rows(nn(hidden, wout)) + ffn_out_bias
    block_out = layer_out.astype(BF)
    third_input, third_gain_part, third_shift_part = norm_back(
        third_back, third_normal, third_inverse, third_gain
    )
    third_grad = out_grad + third_input
    third_grad_low = third_grad.astype(BF)
    tg = gather_rows(third_grad_low)
    ffn_in_grad = tn(pre_grad, third)
    ffn_out_grad = tn(hidden, og)
    ffn_in_bias_grad = jnp.sum(pre_grad.astype(F32), axis=0)

    cross_mixed_grad = nt(tg, cwo).astype(BF)
    cq_grad, ck_part, cv_part = attend_backward(
        cross_queries, cross_keys, cross_values, source, cross_total, cross_mixed_grad
    )
    cq_grad = cq_grad.astype(BF)
    second_back = scatter_rows(scale * nn(cq_grad, cwq))
    second_input, second_gain_part, second_shift_part = norm_back(
        second_back, second_normal, second_inverse, second_gain
    )
    second_grad = third_grad + second_input
    second_grad_low = second_grad.astype(BF)
    sg = gather_rows(second_grad_low)

    def by_core(v):
        v = v.reshape(4, 2, 128, v.shape[-1])
        v = jnp.concatenate([v[:, 0].reshape(512, -1), v[:, 1].reshape(512, -1)], axis=0)
        own = lax.dynamic_slice_in_dim(v, c * 512, 512, 0)
        other = lax.dynamic_slice_in_dim(v, (1 - c) * 512, 512, 0)
        return own, other

    ckv = jnp.concatenate([ck_part, cv_part], axis=1)
    ckv_own, ckv_other = by_core(ckv)
    ckv_grad = (ckv_own + sibling_heads(from_core(ckv_other.astype(BF))).astype(F32)).astype(BF)
    ck_grad, cv_grad = ckv_grad[:, :256], ckv_grad[:, 256:]
    mem_own, _ = by_core(mem)
    memory_part = (nn(ck_grad, cwk) + nn(cv_grad, cwv)).astype(BF)
    memory_grad = scatter_sum(
        [lax.dynamic_slice_in_dim(memory_part, ((y + r) % 4) * 128, 128, 0) for r in range(4)]
    )
    cross_output_grad = tn(cross_mixed, tg)
    cross_query_grad = scale * tn(cq_grad, second)
    ckv_weight_grad = tn(ckv_grad, mem_own)
    cross_query_bias_grad = scale * jnp.sum(cq_grad.astype(F32), axis=0)
    cross_value_bias_grad = jnp.sum(cv_grad.astype(F32), axis=0)

    self_mixed_grad = nt(sg, wo).astype(BF)
    q_grad, k_part, v_part = attend_backward(
        queries, all_keys, all_values, causal, self_total, self_mixed_grad
    )
    q_grad = q_grad.astype(BF)
    kv_part = jnp.concatenate([k_part, v_part], axis=1)
    kv_grad = (kv_part[:512] + sibling_heads(from_core(kv_part[512:].astype(BF))).astype(F32)).astype(BF)
    k_grad, v_grad = kv_grad[:, :256], kv_grad[:, 256:]
    first_back = scatter_rows(scale * nn(q_grad, wq) + nn(k_grad, wk) + nn(v_grad, wv))
    first_input, first_gain_part, first_shift_part = norm_back(
        first_back, first_normal, first_inverse, first_gain
    )
    tokens_grad = second_grad + first_input
    self_output_grad = tn(self_mixed, sg)
    self_query_grad = scale * tn(q_grad, first)
    kv_weight_grad = tn(kv_grad, first)
    self_query_bias_grad = scale * jnp.sum(q_grad.astype(F32), axis=0)
    self_value_bias_grad = jnp.sum(v_grad.astype(F32), axis=0)

    def bias_rows(values):
        n = values.shape[1]
        return jnp.pad(values[:, None, :], ((0, 0), (0, 15), (0, 1024 - n)))

    def pack(matrices, bias):
        parts = [m.reshape(4, -1, 1024) for m in matrices]
        if bias is not None:
            parts.append(bias_rows(bias))
        joined = jnp.concatenate(parts, axis=1)
        return joined.reshape(-1, 1024)

    ffn_sum = grad_sum(pack([ffn_in_grad, ffn_out_grad], ffn_in_bias_grad.reshape(4, 256)))
    cross_sum = grad_sum(
        pack(
            [cross_output_grad, cross_query_grad, ckv_weight_grad[:256], ckv_weight_grad[256:]],
            jnp.concatenate(
                [cross_query_bias_grad.reshape(4, 64), cross_value_bias_grad.reshape(4, 64)], axis=1
            ),
        )
    )
    self_sum = grad_sum(
        pack(
            [self_output_grad, self_query_grad, kv_weight_grad[:256], kv_weight_grad[256:]],
            jnp.concatenate(
                [self_query_bias_grad.reshape(4, 64), self_value_bias_grad.reshape(4, 64)], axis=1
            ),
        )
    )
    vectors = whole_sum(
        jnp.stack(
            [
                first_gain_part,
                first_shift_part,
                second_gain_part,
                second_shift_part,
                third_gain_part,
                third_shift_part,
                jnp.sum(out_grad_low.astype(F32), axis=0),
                jnp.sum(third_grad_low.astype(F32), axis=0),
                jnp.sum(second_grad_low.astype(F32), axis=0),
            ]
        )
    )
    return (
        block_out,
        tokens_grad,
        memory_grad,
        vectors[0],
        vectors[1],
        self_sum[64:128].T,
        self_sum[256, :64],
        self_sum[128:192].T,
        self_sum[192:256].T,
        self_sum[256, 64:128],
        self_sum[:64],
        vectors[8],
        vectors[2],
        vectors[3],
        cross_sum[64:128].T,
        cross_sum[256, :64],
        cross_sum[128:192].T,
        cross_sum[192:256].T,
        cross_sum[256, 64:128],
        cross_sum[:64],
        vectors[7],
        vectors[4],
        vectors[5],
        ffn_sum[:256].T,
        ffn_sum[512, :256],
        ffn_sum[256:512],
        vectors[6],
    )


def solution(mesh):
    fine = Mesh(mesh.devices.reshape(4, 2, 2, 4, 2), ("x", "zl", "zh", "y", "c"))
    dp = ("x", "zl")
    mp = ("zh", "y", "c")
    rows = P(dp + mp, None)
    cols = P(None, mp)
    part = P(mp)
    down = P(mp, None)
    whole = P()
    placed = (
        rows,
        P(dp, None),
        rows,
        P(dp),
        P(dp),
        P(dp),
        whole,
        whole,
        whole,
        cols,
        part,
        cols,
        cols,
        part,
        down,
        whole,
        whole,
        whole,
        cols,
        part,
        cols,
        cols,
        part,
        down,
        whole,
        whole,
        whole,
        cols,
        part,
        down,
        whole,
    )
    given = (
        rows,
        rows,
        rows,
        whole,
        whole,
        cols,
        part,
        cols,
        cols,
        part,
        down,
        whole,
        whole,
        whole,
        cols,
        part,
        cols,
        cols,
        part,
        down,
        whole,
        whole,
        whole,
        cols,
        part,
        down,
        whole,
    )
    return jax.shard_map(per_device, mesh=fine, in_specs=placed, out_specs=given, check_vma=False)
```

time: 1250 us -> 464 us (0.37)
  waiting for transfers between devices: 925 us -> 129 us
  starting transfers between devices: 2.02 us -> 110 us
  blocking collectives: 84.5 us -> 0 us
  local copies, waits for them, and re-layouts: 22 us -> 96 us
  matrix products: 112 us -> 56 us
  other arithmetic: 76 us -> 58.4 us
    reduce_scatter x6 -> x0, waiting for transfers between devices: 426 us -> none  [the longest x1 81.2 us: per_device(): lax.psum_scatter(matmul(hidden_low, ffn_out).astype(jnp.bfloat16), 'mp',...]
    all_gather x5 -> x0, waiting for transfers between devices: 257 us -> none  [the longest x1 61.1 us: per_device(): lax.all_gather(tokens, 'mp', axis=0, tiled=True).astype(jnp.float32)]
    psum x2 -> x0, waiting for transfers between devices: 240 us -> none  [the longest x1 154 us: per_device(): lax.psum(matmul(self_mixed, self_output), 'mp') + self_output_bias]
    ppermute x0 -> x82, waiting for transfers between devices: none -> 125 us  [the longest x30 51.9 us: scatter_sum(): got = [lax.ppermute(blocks[r], axis, ring(4, r)) for r in range(1, 4)]]
    ppermute x0 -> x82, starting transfers between devices: none -> 101 us  [the longest x30 39.7 us: scatter_sum(): got = [lax.ppermute(blocks[r], axis, ring(4, r)) for r in range(1, 4)]]
    psum x2 -> x0, blocking collectives: 84.5 us -> none  [the longest x1 65 us: per_device(): lax.psum((first_gain_part, first_shift_part, second_gain_part, second_shi...]
    dot_general x58 -> x40, matrix products: 112 us -> 56 us  [the longest x10 15 us: nt(): lax.dot_general(a, b, (((1,), (1,)), ((), ())), preferred_element_type=F32)]
    slice x0 -> x30, local copies, waits for them, and re-layouts: none -> 28.7 us  [the longest x7 12.7 us: grad_sum(): mine = parts[:2 * rows] + from_core(low[2 * rows:]).astype(F32)]
  transfers between devices with their start and end apart: 13 -> 84, of which waited for: 13 -> 37; matrix products, arithmetic and copies ran while one was open for 9% -> 39% of each run, Pallas kernels for 0% -> 0%
where the time goes in v1:
time: 464 us; the launch traced here: 456 us
  waiting for transfers between devices  129 us (28%)
  starting transfers between devices  110 us (24%)
  local copies, waits for them, and re-layouts  96 us (21%)
  other arithmetic  58.4 us (13%)
  matrix products  56 us (12%)
  between operations  6.69 us (1%)
    ppermute x30, waiting for transfers between devices, scatter_sum(): got = [lax.ppermute(blocks[r], axis, ring(4, r)) for r in range(1, 4)]  51.9 us
    ppermute x27, waiting for transfers between devices, gather_rel(): return [v] + [lax.ppermute(v, axis, ring(4, 4 - r)) for r in range(1, 4)]  42.5 us
    ppermute x30, starting transfers between devices, scatter_sum(): got = [lax.ppermute(blocks[r], axis, ring(4, r)) for r in range(1, 4)]  39.7 us
    ppermute x27, starting transfers between devices, gather_rel(): return [v] + [lax.ppermute(v, axis, ring(4, 4 - r)) for r in range(1, 4)]  36 us
    unnamed x347, local copies, waits for them, and re-layouts  33.2 us
    ppermute x8, starting transfers between devices, from_half(): return lax.ppermute(v, ('zl', 'zh'), [(i, 3 - i) for i in range(4)])  15.7 us
    ppermute x6, waiting for transfers between devices, from_zl(): return lax.ppermute(v, 'zl', ring(2, 1))  15.3 us
    dot_general x10, matrix products, nt(): lax.dot_general(a, b, (((1,), (1,)), ((), ())), preferred_element_type=F32)  15 us
  transfers between devices with their start and end apart: 84, of which 37 were waited for; matrix products, arithmetic and copies ran while one was open for 39% of the time, Pallas kernels for 0%

profile of v1, /device:TPU:0, one launch (start us, length us, event | category | flops | bytes accessed | tf_op | source)
XLA Modules:
  0.0 456.5 jit_solution(13590000549546476484)
XLA Ops:
  1.6 4.1 collective-permute-start.5
  18.8 3.2 collective-permute-start.8
  39.0 3.2 collective-permute-start.22
  50.5 8.2 %collective-permute-done.22 = bf16[256,1024]{0,1:T(8,128)(2,1)} collective-permute-done((bf16[256,1024]{0,1:T(8,128)(2,1)}, bf16[256,1024]{0,1:T(8,128)(2,1)}, u32[]{:S(2)}, u32[]{:S(2)}) %collective-permute-start.22) | collective-permute-done | bytes 524320 | tf_op jit(solution)/shard_map/ppermute | solution.py:32
  58.7 2.9 collective-permute-start.1
  68.3 3.5 collective-permute-done
  86.7 2.7 collective-permute-start.12
  92.1 9.1 %collective-permute-done.12 = bf16[128,1024]{1,0:T(8,128)(2,1)S(1)} collective-permute-done((bf16[128,1024]{1,0:T(8,128)(2,1)S(1)}, bf16[128,1024]{1,0:T(8,128)(2,1)S(1)}, u32[]{:S(2)}, u32[]{:S(2)}) %collective-permute-start.12) | collective-permute-done | bytes 262176 | tf_op jit(solution)/shard_map/ppermute | solution.py:52
  101.3 3.7 collective-permute-done.10
  107.8 2.7 collective-permute-start.13
  111.4 9.4 %collective-permute-done.15 = bf16[128,1024]{1,0:T(8,128)(2,1)S(1)} collective-permute-done((bf16[128,1024]{1,0:T(8,128)(2,1)S(1)}, bf16[128,1024]{1,0:T(8,128)(2,1)S(1)}, u32[]{:S(2)}, u32[]{:S(2)}) %collective-permute-start.15) | collective-permute-done | bytes 262176 | tf_op jit(solution)/shard_map/ppermute | solution.py:44
  128.4 2.6 collective-permute-start.18
  133.3 9.2 %collective-permute-done.18 = bf16[128,1024]{1,0:T(8,128)(2,1)S(1)} collective-permute-done((bf16[128,1024]{1,0:T(8,128)(2,1)S(1)}, bf16[128,1024]{1,0:T(8,128)(2,1)S(1)}, u32[]{:S(2)}, u32[]{:S(2)}) %collective-permute-start.18) | collective-permute-done | bytes 262176 | tf_op jit(solution)/shard_map/ppermute | solution.py:52
  142.4 3.6 collective-permute-done.16
  150.0 3.0 collective-permute-start.30
  153.1 14.2 %collective-permute-done.21 = bf16[128,1024]{1,0:T(8,128)(2,1)S(1)} collective-permute-done((bf16[128,1024]{1,0:T(8,128)(2,1)S(1)}, bf16[128,1024]{1,0:T(8,128)(2,1)S(1)}, u32[]{:S(2)}, u32[]{:S(2)}) %collective-permute-start.21) | collective-permute-done | bytes 262176 | tf_op jit(solution)/shard_map/ppermute | solution.py:44
  171.4 3.3 collective-permute-done.29
  174.7 3.8 convert_reduce_fusion
  191.1 3.2 collective-permute-done.34
  194.5 4.4 collective-permute-done.32
  199.8 3.7 collective-permute-done.28
  204.4 2.8 collective-permute-done.26
  214.1 3.4 copy-done.1
  219.3 4.0 collective-permute-done.37
  232.0 2.6 fusion.23
  237.0 2.6 collective-permute-start.40
  244.3 3.1 concatenate.175
  249.0 6.1 %slice_reduce_fusion = (f32[4,128,512]{1,0,2:T(4,128)S(1)}, f32[4,128,512]{1,0,2:T(4,128)S(1)}) fusion(f32[4,2,128,512]{2,1,0,3:T(2,128)S(1)} %constant_dynamic-update-slice_fusion.14), kind=kLoop, calls=%fused_computation.99 | loop fusion | bytes 4194304 | tf_op jit(solution)/shard_map/slice | solution.py:289
  258.8 2.6 multiply_reduce_fusion.3
  263.1 2.7 collective-permute-start.43
  277.8 3.0 slice.653
  286.9 3.0 multiply_reduce_fusion
  308.0 3.2 collective-permute-start.47
  318.3 3.3 slice.575
  321.6 2.9 slice.654
  326.8 2.8 fusion.56
  330.8 3.7 all-to-all-start
  337.4 4.2 collective-permute-start.63
  341.6 2.7 bitcast_add_fusion
  348.2 4.2 all-to-all-done
  353.4 5.6 %all-to-all-start.1 = ((f32[8,9,1024]{2,1,0:T(8,128)}), f32[8,9,1024]{2,1,0:T(8,128)S(1)}, u32[]{:S(2)}, u32[]{:S(2)}) async-start(f32[8,9,1024]{2,1,0:T(8,128)} %broadcast_in_dim.53), calls=%async_computation.1 | async-start | bytes 1048576 | tf_op jit(solution)/shard_map/all_to_all | solution.py:68
  358.9 3.4 collective-permute-done.63
  370.0 3.9 collective-permute-done.64
  380.9 2.7 collective-permute-done.66
  403.3 4.9 %collective-permute-done.54 = bf16[136,1024]{1,0:T(8,128)(2,1)S(1)} collective-permute-done((bf16[136,1024]{1,0:T(8,128)(2,1)S(1)}, bf16[136,1024]{1,0:T(8,128)(2,1)S(1)}, u32[]{:S(2)}, u32[]{:S(2)}) %collective-permute-start.54) | collective-permute-done | bytes 278560 | tf_op jit(solution)/shard_map/ppermute | solution.py:36
  408.4 2.8 collective-permute-start.57
  413.8 3.4 collective-permute-done.56
  446.3 6.4 %collective-permute-done.81 = bf16[264,1024]{1,0:T(8,128)(2,1)S(1)} collective-permute-done((bf16[264,1024]{1,0:T(8,128)(2,1)S(1)}, bf16[264,1024]{1,0:T(8,128)(2,1)S(1)}, u32[]{:S(2)}, u32[]{:S(2)}) %collective-permute-start.81) | collective-permute-done | bytes 540704 | tf_op jit(solution)/shard_map/ppermute | solution.py:36
  (673 shorter events, 250.0 us)
Async XLA Ops:
  1.6 35.4 %collective-permute-start.5 = (f32[1,512]{1,0:T(1,128)S(1)}, f32[1,512]{1,0:T(1,128)}, u32[]{:S(2)}, u32[]{:S(2)}) collective-permute-start(f32[1,512]{1,0:T(1,128)S(1)} %bitcast.246), channel_id=1, source_target_pairs={{0,24},{8,16},{16,8},{24,0},{1,25},{9,17},{17,9},{25,1},{2,26},{10... | collective-permute-start | bytes 6152 | tf_op jit(solution)/shard_map/ppermute | solution.py:32
  7.5 40.6 %collective-permute-start.3 = (bf16[192,1024]{1,0:T(8,128)(2,1)}, bf16[192,1024]{1,0:T(8,128)(2,1)}, u32[]{:S(2)}, u32[]{:S(2)}) collective-permute-start(bf16[192,1024]{1,0:T(8,128)(2,1)} %pad_maximum_fusion.22), channel_id=1, source_target_pairs={{0,24},{8,16},{16,8},{24,0},{1,25},{9,17},{17,9},{25,1},{2,26},{10... | collective-permute-start | bytes 1179656 | tf_op jit(solution)/shard_map/ppermute | solution.py:32
  11.8 54.7 %collective-permute-start.2 = (bf16[128,1024]{1,0:T(8,128)(2,1)}, bf16[128,1024]{1,0:T(8,128)(2,1)}, u32[]{:S(2)}, u32[]{:S(2)}) collective-permute-start(bf16[128,1024]{1,0:T(8,128)(2,1)} %fusion.51), channel_id=1, source_target_pairs={{0,2},{2,4},{4,6},{6,0},{1,3},{3,5},{5,7},{7,1},{8,10},{10,12},{12... | collective-permute-start | bytes 786440 | tf_op jit(solution)/shard_map/ppermute | solution.py:44
  18.8 46.6 %collective-permute-start.8 = (bf16[320,1024]{1,0:T(8,128)(2,1)}, bf16[320,1024]{1,0:T(8,128)(2,1)S(1)}, u32[]{:S(2)}, u32[]{:S(2)}) collective-permute-start(bf16[320,1024]{1,0:T(8,128)(2,1)} %get-tuple-element.228), channel_id=1, source_target_pairs={{0,24},{8,16},{16,8},{24,0},{1,25},{9,17},{17,9},{25,1},{2,26},{10... | collective-permute-start | bytes 1966088 | tf_op jit(solution)/shard_map/ppermute | solution.py:32
  22.1 40.7 %collective-permute-start.24 = (bf16[256,1024]{1,0:T(8,128)(2,1)}, bf16[256,1024]{1,0:T(8,128)(2,1)}, u32[]{:S(2)}, u32[]{:S(2)}) collective-permute-start(bf16[256,1024]{1,0:T(8,128)(2,1)} %param.60), channel_id=1, source_target_pairs={{0,24},{8,16},{16,8},{24,0},{1,25},{9,17},{17,9},{25,1},{2,26},{10... | collective-permute-start | bytes 1572872 | tf_op jit(solution)/shard_map/ppermute | solution.py:32
  39.0 19.7 %collective-permute-start.22 = (bf16[256,1024]{0,1:T(8,128)(2,1)}, bf16[256,1024]{0,1:T(8,128)(2,1)}, u32[]{:S(2)}, u32[]{:S(2)}) collective-permute-start(bf16[256,1024]{0,1:T(8,128)(2,1)} %bitcast.238), channel_id=1, source_target_pairs={{0,24},{8,16},{16,8},{24,0},{1,25},{9,17},{17,9},{25,1},{2,26},{10... | collective-permute-start | bytes 1572872 | tf_op jit(solution)/shard_map/ppermute | solution.py:32
  49.3 17.0 %collective-permute-start.4 = (bf16[384,1024]{1,0:T(8,128)(2,1)S(1)}, bf16[384,1024]{1,0:T(8,128)(2,1)S(1)}, u32[]{:S(2)}, u32[]{:S(2)}) collective-permute-start(bf16[384,1024]{1,0:T(8,128)(2,1)S(1)} %pad_maximum_fusion.12), channel_id=1, source_target_pairs={{0,1},{1,0},{2,3},{3,2},{4,5},{5,4},{6,7},{7,6},{8,9},{9,8},{10,11... | collective-permute-start | bytes 2359304 | tf_op jit(solution)/shard_map/ppermute | solution.py:28
  65.5 105.9 %collective-permute-start.31 = (bf16[128,1024]{1,0:T(8,128)(2,1)S(1)}, bf16[128,1024]{1,0:T(8,128)(2,1)S(1)}, u32[]{:S(2)}, u32[]{:S(2)}) collective-permute-start(bf16[128,1024]{1,0:T(8,128)(2,1)S(1)} %copy-done.73), channel_id=1, source_target_pairs={{0,2},{2,4},{4,6},{6,0},{1,3},{3,5},{5,7},{7,1},{8,10},{10,12},{12... | collective-permute-start | bytes 786440 | tf_op jit(solution)/shard_map/ppermute | solution.py:44
  66.3 66.8 %collective-permute-start.25 = (bf16[512,1024]{1,0:T(8,128)(2,1)S(1)}, bf16[512,1024]{1,0:T(8,128)(2,1)S(1)}, u32[]{:S(2)}, u32[]{:S(2)}) collective-permute-start(bf16[512,1024]{1,0:T(8,128)(2,1)S(1)} %pad_maximum_fusion.6), channel_id=1, source_target_pairs={{0,1},{1,0},{2,3},{3,2},{4,5},{5,4},{6,7},{7,6},{8,9},{9,8},{10,11... | collective-permute-start | bytes 3145736 | tf_op jit(solution)/shard_map/ppermute | solution.py:28
  66.5 18.6 %collective-permute-start.9 = (bf16[640,1024]{1,0:T(8,128)(2,1)S(1)}, bf16[640,1024]{1,0:T(8,128)(2,1)S(1)}, u32[]{:S(2)}, u32[]{:S(2)}) collective-permute-start(bf16[640,1024]{1,0:T(8,128)(2,1)S(1)} %constant_dynamic-update-slice_fusion.5), channel_id=1, source_target_pairs={{0,1},{1,0},{2,3},{3,2},{4,5},{5,4},{6,7},{7,6},{8,9},{9,8},{10,11... | collective-permute-start | bytes 3932168 | tf_op jit(solution)/shard_map/ppermute | solution.py:28
  86.7 14.6 %collective-permute-start.12 = (bf16[128,1024]{1,0:T(8,128)(2,1)S(1)}, bf16[128,1024]{1,0:T(8,128)(2,1)S(1)}, u32[]{:S(2)}, u32[]{:S(2)}) collective-permute-start(bf16[128,1024]{1,0:T(8,128)(2,1)S(1)} %get-tuple-element.180), channel_id=1, source_target_pairs={{0,6},{2,0},{4,2},{6,4},{1,7},{3,1},{5,3},{7,5},{8,14},{10,8},{12,... | collective-permute-start | bytes 786440 | tf_op jit(solution)/shard_map/ppermute | solution.py:52
  91.2 13.7 %collective-permute-start.10 = (bf16[128,1024]{1,0:T(8,128)(2,1)S(1)}, bf16[128,1024]{1,0:T(8,128)(2,1)S(1)}, u32[]{:S(2)}, u32[]{:S(2)}) collective-permute-start(bf16[128,1024]{1,0:T(8,128)(2,1)S(1)} %get-tuple-element.179), channel_id=1, source_target_pairs={{0,2},{2,4},{4,6},{6,0},{1,3},{3,5},{5,7},{7,1},{8,10},{10,12},{12... | collective-permute-start | bytes 786440 | tf_op jit(solution)/shard_map/ppermute | solution.py:52
  105.7 15.1 %collective-permute-start.15 = (bf16[128,1024]{1,0:T(8,128)(2,1)S(1)}, bf16[128,1024]{1,0:T(8,128)(2,1)S(1)}, u32[]{:S(2)}, u32[]{:S(2)}) collective-permute-start(bf16[128,1024]{1,0:T(8,128)(2,1)S(1)} %add_convert_fusion.8), channel_id=1, source_target_pairs={{0,2},{2,4},{4,6},{6,0},{1,3},{3,5},{5,7},{7,1},{8,10},{10,12},{12... | collective-permute-start | bytes 786440 | tf_op jit(solution)/shard_map/ppermute | solution.py:44
  106.1 14.7 %collective-permute-start.14 = (bf16[128,1024]{1,0:T(8,128)(2,1)S(1)}, bf16[128,1024]{1,0:T(8,128)(2,1)S(1)}, u32[]{:S(2)}, u32[]{:S(2)}) collective-permute-start(bf16[128,1024]{1,0:T(8,128)(2,1)S(1)} %add_convert_fusion.8), channel_id=1, source_target_pairs={{0,4},{2,6},{4,0},{6,2},{1,5},{3,7},{5,1},{7,3},{8,12},{10,14},{12... | collective-permute-start | bytes 786440 | tf_op jit(solution)/shard_map/ppermute | solution.py:44
  107.8 13.6 %collective-permute-start.13 = (bf16[128,1024]{1,0:T(8,128)(2,1)S(1)}, bf16[128,1024]{1,0:T(8,128)(2,1)S(1)}, u32[]{:S(2)}, u32[]{:S(2)}) collective-permute-start(bf16[128,1024]{1,0:T(8,128)(2,1)S(1)} %add_convert_fusion.8), channel_id=1, source_target_pairs={{0,6},{2,0},{4,2},{6,4},{1,7},{3,1},{5,3},{7,5},{8,14},{10,8},{12,... | collective-permute-start | bytes 786440 | tf_op jit(solution)/shard_map/ppermute | solution.py:44
  128.4 14.0 %collective-permute-start.18 = (bf16[128,1024]{1,0:T(8,128)(2,1)S(1)}, bf16[128,1024]{1,0:T(8,128)(2,1)S(1)}, u32[]{:S(2)}, u32[]{:S(2)}) collective-permute-start(bf16[128,1024]{1,0:T(8,128)(2,1)S(1)} %get-tuple-element.177), channel_id=1, source_target_pairs={{0,6},{2,0},{4,2},{6,4},{1,7},{3,1},{5,3},{7,5},{8,14},{10,8},{12,... | collective-permute-start | bytes 786440 | tf_op jit(solution)/shard_map/ppermute | solution.py:52
  131.5 14.5 %collective-permute-start.16 = (bf16[128,1024]{1,0:T(8,128)(2,1)S(1)}, bf16[128,1024]{1,0:T(8,128)(2,1)S(1)}, u32[]{:S(2)}, u32[]{:S(2)}) collective-permute-start(bf16[128,1024]{1,0:T(8,128)(2,1)S(1)} %get-tuple-element.176), channel_id=1, source_target_pairs={{0,2},{2,4},{4,6},{6,0},{1,3},{3,5},{5,7},{7,1},{8,10},{10,12},{12... | collective-permute-start | bytes 786440 | tf_op jit(solution)/shard_map/ppermute | solution.py:52
  133.1 16.9 %collective-permute-start.23 = (bf16[512,1024]{0,1:T(8,128)(2,1)S(1)}, bf16[512,1024]{0,1:T(8,128)(2,1)S(1)}, u32[]{:S(2)}, u32[]{:S(2)}) collective-permute-start(bf16[512,1024]{0,1:T(8,128)(2,1)S(1)} %pad_maximum_fusion.5), channel_id=1, source_target_pairs={{0,1},{1,0},{2,3},{3,2},{4,5},{5,4},{6,7},{7,6},{8,9},{9,8},{10,11... | collective-permute-start | bytes 3145736 | tf_op jit(solution)/shard_map/ppermute | solution.py:28
  146.7 20.6 %collective-permute-start.21 = (bf16[128,1024]{1,0:T(8,128)(2,1)S(1)}, bf16[128,1024]{1,0:T(8,128)(2,1)S(1)}, u32[]{:S(2)}, u32[]{:S(2)}) collective-permute-start(bf16[128,1024]{1,0:T(8,128)(2,1)S(1)} %add_convert_fusion.7), channel_id=1, source_target_pairs={{0,2},{2,4},{4,6},{6,0},{1,3},{3,5},{5,7},{7,1},{8,10},{10,12},{12... | collective-permute-start | bytes 786440 | tf_op jit(solution)/shard_map/ppermute | solution.py:44
  146.8 20.7 %collective-permute-start.20 = (bf16[128,1024]{1,0:T(8,128)(2,1)S(1)}, bf16[128,1024]{1,0:T(8,128)(2,1)S(1)}, u32[]{:S(2)}, u32[]{:S(2)}) collective-permute-start(bf16[128,1024]{1,0:T(8,128)(2,1)S(1)} %add_convert_fusion.7), channel_id=1, source_target_pairs={{0,4},{2,6},{4,0},{6,2},{1,5},{3,7},{5,1},{7,3},{8,12},{10,14},{12... | collective-permute-start | bytes 786440 | tf_op jit(solution)/shard_map/ppermute | solution.py:44
  149.0 18.5 %collective-permute-start.19 = (bf16[128,1024]{1,0:T(8,128)(2,1)S(1)}, bf16[128,1024]{1,0:T(8,128)(2,1)S(1)}, u32[]{:S(2)}, u32[]{:S(2)}) collective-permute-start(bf16[128,1024]{1,0:T(8,128)(2,1)S(1)} %add_convert_fusion.7), channel_id=1, source_target_pairs={{0,6},{2,0},{4,2},{6,4},{1,7},{3,1},{5,3},{7,5},{8,14},{10,8},{12,... | collective-permute-start | bytes 786440 | tf_op jit(solution)/shard_map/ppermute | solution.py:44
  150.0 21.3 %collective-permute-start.30 = (bf16[128,1024]{1,0:T(8,128)(2,1)S(1)}, bf16[128,1024]{1,0:T(8,128)(2,1)S(1)}, u32[]{:S(2)}, u32[]{:S(2)}) collective-permute-start(bf16[128,1024]{1,0:T(8,128)(2,1)S(1)} %copy-done.73), channel_id=1, source_target_pairs={{0,4},{2,6},{4,0},{6,2},{1,5},{3,7},{5,1},{7,3},{8,12},{10,14},{12... | collective-permute-start | bytes 786440 | tf_op jit(solution)/shard_map/ppermute | solution.py:44
  180.9 13.5 %collective-permute-start.34 = (bf16[128,1024]{1,0:T(8,128)(2,1)S(1)}, bf16[128,1024]{1,0:T(8,128)(2,1)S(1)}, u32[]{:S(2)}, u32[]{:S(2)}) collective-permute-start(bf16[128,1024]{1,0:T(8,128)(2,1)S(1)} %get-tuple-element.171), channel_id=1, source_target_pairs={{0,6},{2,0},{4,2},{6,4},{1,7},{3,1},{5,3},{7,5},{8,14},{10,8},{12,... | collective-permute-start | bytes 786440 | tf_op jit(solution)/shard_map/ppermute | solution.py:52
  182.6 16.3 %collective-permute-start.32 = (bf16[128,1024]{1,0:T(8,128)(2,1)S(1)}, bf16[128,1024]{1,0:T(8,128)(2,1)S(1)}, u32[]{:S(2)}, u32[]{:S(2)}) collective-permute-start(bf16[128,1024]{1,0:T(8,128)(2,1)S(1)} %get-tuple-element.170), channel_id=1, source_target_pairs={{0,2},{2,4},{4,6},{6,0},{1,3},{3,5},{5,7},{7,1},{8,10},{10,12},{12... | collective-permute-start | bytes 786440 | tf_op jit(solution)/shard_map/ppermute | solution.py:52
  183.5 20.0 %collective-permute-start.28 = (bf16[128,1024]{1,0:T(8,128)(2,1)S(1)}, bf16[128,1024]{1,0:T(8,128)(2,1)S(1)}, u32[]{:S(2)}, u32[]{:S(2)}) collective-permute-start(bf16[128,1024]{1,0:T(8,128)(2,1)S(1)} %get-tuple-element.174), channel_id=1, source_target_pairs={{0,6},{2,0},{4,2},{6,4},{1,7},{3,1},{5,3},{7,5},{8,14},{10,8},{12,... | collective-permute-start | bytes 786440 | tf_op jit(solution)/shard_map/ppermute | solution.py:52
  185.9 18.5 %collective-permute-start.27 = (bf16[128,1024]{1,0:T(8,128)(2,1)S(1)}, bf16[128,1024]{1,0:T(8,128)(2,1)S(1)}, u32[]{:S(2)}, u32[]{:S(2)}) collective-permute-start(bf16[128,1024]{1,0:T(8,128)(2,1)S(1)} %get-tuple-element.175), channel_id=1, source_target_pairs={{0,4},{2,6},{4,0},{6,2},{1,5},{3,7},{5,1},{7,3},{8,12},{10,14},{12... | collective-permute-start | bytes 786440 | tf_op jit(solution)/shard_map/ppermute | solution.py:52
  209.1 14.2 %collective-permute-start.37 = (bf16[128,1024]{1,0:T(8,128)(2,1)S(1)}, bf16[128,1024]{1,0:T(8,128)(2,1)S(1)}, u32[]{:S(2)}, u32[]{:S(2)}) collective-permute-start(bf16[128,1024]{1,0:T(8,128)(2,1)S(1)} %get-tuple-element.126), channel_id=1, source_target_pairs={{0,2},{2,4},{4,6},{6,0},{1,3},{3,5},{5,7},{7,1},{8,10},{10,12},{12... | collective-permute-start | bytes 786440 | tf_op jit(solution)/shard_map/ppermute | solution.py:44
  209.1 14.2 %collective-permute-start.36 = (bf16[128,1024]{1,0:T(8,128)(2,1)S(1)}, bf16[128,1024]{1,0:T(8,128)(2,1)S(1)}, u32[]{:S(2)}, u32[]{:S(2)}) collective-permute-start(bf16[128,1024]{1,0:T(8,128)(2,1)S(1)} %get-tuple-element.126), channel_id=1, source_target_pairs={{0,4},{2,6},{4,0},{6,2},{1,5},{3,7},{5,1},{7,3},{8,12},{10,14},{12... | collective-permute-start | bytes 786440 | tf_op jit(solution)/shard_map/ppermute | solution.py:44
  219.1 122.5 %collective-permute-start.72 = (bf16[1056,1024]{1,0:T(8,128)(2,1)}, bf16[1056,1024]{1,0:T(8,128)(2,1)}, u32[]{:S(2)}, u32[]{:S(2)}) collective-permute-start(bf16[1056,1024]{1,0:T(8,128)(2,1)} %bitcast.92), channel_id=1, source_target_pairs={{0,1},{1,0},{2,3},{3,2},{4,5},{5,4},{6,7},{7,6},{8,9},{9,8},{10,11... | collective-permute-start | bytes 6488072 | tf_op jit(solution)/shard_map/ppermute | solution.py:28
  237.0 21.8 %collective-permute-start.40 = (bf16[128,1024]{1,0:T(8,128)(2,1)}, bf16[128,1024]{1,0:T(8,128)(2,1)}, u32[]{:S(2)}, u32[]{:S(2)}) collective-permute-start(bf16[128,1024]{1,0:T(8,128)(2,1)} %get-tuple-element.168), channel_id=1, source_target_pairs={{0,6},{2,0},{4,2},{6,4},{1,7},{3,1},{5,3},{7,5},{8,14},{10,8},{12,... | collective-permute-start | bytes 786440 | tf_op jit(solution)/shard_map/ppermute | solution.py:52
  239.6 19.2 %collective-permute-start.39 = (bf16[128,1024]{1,0:T(8,128)(2,1)}, bf16[128,1024]{1,0:T(8,128)(2,1)}, u32[]{:S(2)}, u32[]{:S(2)}) collective-permute-start(bf16[128,1024]{1,0:T(8,128)(2,1)} %get-tuple-element.169), channel_id=1, source_target_pairs={{0,4},{2,6},{4,0},{6,2},{1,5},{3,7},{5,1},{7,3},{8,12},{10,14},{12... | collective-permute-start | bytes 786440 | tf_op jit(solution)/shard_map/ppermute | solution.py:52
  240.4 18.3 %collective-permute-start.38 = (bf16[128,1024]{1,0:T(8,128)(2,1)}, bf16[128,1024]{1,0:T(8,128)(2,1)}, u32[]{:S(2)}, u32[]{:S(2)}) collective-permute-start(bf16[128,1024]{1,0:T(8,128)(2,1)} %get-tuple-element.167), channel_id=1, source_target_pairs={{0,2},{2,4},{4,6},{6,0},{1,3},{3,5},{5,7},{7,1},{8,10},{10,12},{12... | collective-permute-start | bytes 786440 | tf_op jit(solution)/shard_map/ppermute | solution.py:52
  263.1 19.9 %collective-permute-start.43 = (bf16[128,1024]{1,0:T(8,128)(2,1)}, bf16[128,1024]{1,0:T(8,128)(2,1)}, u32[]{:S(2)}, u32[]{:S(2)}) collective-permute-start(bf16[128,1024]{1,0:T(8,128)(2,1)} %get-tuple-element.123), channel_id=1, source_target_pairs={{0,2},{2,4},{4,6},{6,0},{1,3},{3,5},{5,7},{7,1},{8,10},{10,12},{12... | collective-permute-start | bytes 786440 | tf_op jit(solution)/shard_map/ppermute | solution.py:44
  265.8 19.3 %collective-permute-start.42 = (bf16[128,1024]{1,0:T(8,128)(2,1)}, bf16[128,1024]{1,0:T(8,128)(2,1)}, u32[]{:S(2)}, u32[]{:S(2)}) collective-permute-start(bf16[128,1024]{1,0:T(8,128)(2,1)} %get-tuple-element.123), channel_id=1, source_target_pairs={{0,4},{2,6},{4,0},{6,2},{1,5},{3,7},{5,1},{7,3},{8,12},{10,14},{12... | collective-permute-start | bytes 786440 | tf_op jit(solution)/shard_map/ppermute | solution.py:44
  267.8 17.3 %collective-permute-start.41 = (bf16[128,1024]{1,0:T(8,128)(2,1)}, bf16[128,1024]{1,0:T(8,128)(2,1)}, u32[]{:S(2)}, u32[]{:S(2)}) collective-permute-start(bf16[128,1024]{1,0:T(8,128)(2,1)} %get-tuple-element.123), channel_id=1, source_target_pairs={{0,6},{2,0},{4,2},{6,4},{1,7},{3,1},{5,3},{7,5},{8,14},{10,8},{12,... | collective-permute-start | bytes 786440 | tf_op jit(solution)/shard_map/ppermute | solution.py:44
  281.7 20.5 %collective-permute-start.51 = (bf16[128,1024]{1,0:T(8,128)(2,1)}, bf16[128,1024]{1,0:T(8,128)(2,1)}, u32[]{:S(2)}, u32[]{:S(2)}) collective-permute-start(bf16[128,1024]{1,0:T(8,128)(2,1)} %get-tuple-element.162), channel_id=1, source_target_pairs={{0,6},{2,0},{4,2},{6,4},{1,7},{3,1},{5,3},{7,5},{8,14},{10,8},{12,... | collective-permute-start | bytes 786440 | tf_op jit(solution)/shard_map/ppermute | solution.py:52
  283.0 19.3 %collective-permute-start.50 = (bf16[128,1024]{1,0:T(8,128)(2,1)}, bf16[128,1024]{1,0:T(8,128)(2,1)}, u32[]{:S(2)}, u32[]{:S(2)}) collective-permute-start(bf16[128,1024]{1,0:T(8,128)(2,1)} %get-tuple-element.163), channel_id=1, source_target_pairs={{0,4},{2,6},{4,0},{6,2},{1,5},{3,7},{5,1},{7,3},{8,12},{10,14},{12... | collective-permute-start | bytes 786440 | tf_op jit(solution)/shard_map/ppermute | solution.py:52
  285.1 17.3 %collective-permute-start.49 = (bf16[128,1024]{1,0:T(8,128)(2,1)}, bf16[128,1024]{1,0:T(8,128)(2,1)}, u32[]{:S(2)}, u32[]{:S(2)}) collective-permute-start(bf16[128,1024]{1,0:T(8,128)(2,1)} %get-tuple-element.161), channel_id=1, source_target_pairs={{0,2},{2,4},{4,6},{6,0},{1,3},{3,5},{5,7},{7,1},{8,10},{10,12},{12... | collective-permute-start | bytes 786440 | tf_op jit(solution)/shard_map/ppermute | solution.py:52
  302.2 32.3 %collective-permute-start.62 = (bf16[544,1024]{1,0:T(8,128)(2,1)}, bf16[544,1024]{1,0:T(8,128)(2,1)}, u32[]{:S(2)}, u32[]{:S(2)}) collective-permute-start(bf16[544,1024]{1,0:T(8,128)(2,1)} %bitcast.79), channel_id=1, source_target_pairs={{0,1},{1,0},{2,3},{3,2},{4,5},{5,4},{6,7},{7,6},{8,9},{9,8},{10,11... | collective-permute-start | bytes 3342344 | tf_op jit(solution)/shard_map/ppermute | solution.py:28
  308.0 16.5 %collective-permute-start.47 = (bf16[128,1024]{1,0:T(8,128)(2,1)}, bf16[128,1024]{1,0:T(8,128)(2,1)}, u32[]{:S(2)}, u32[]{:S(2)}) collective-permute-start(bf16[128,1024]{1,0:T(8,128)(2,1)} %get-tuple-element.165), channel_id=1, source_target_pairs={{0,6},{2,0},{4,2},{6,4},{1,7},{3,1},{5,3},{7,5},{8,14},{10,8},{12,... | collective-permute-start | bytes 786440 | tf_op jit(solution)/shard_map/ppermute | solution.py:52
  311.5 15.3 %collective-permute-start.45 = (bf16[128,1024]{1,0:T(8,128)(2,1)}, bf16[128,1024]{1,0:T(8,128)(2,1)}, u32[]{:S(2)}, u32[]{:S(2)}) collective-permute-start(bf16[128,1024]{1,0:T(8,128)(2,1)} %get-tuple-element.164), channel_id=1, source_target_pairs={{0,2},{2,4},{4,6},{6,0},{1,3},{3,5},{5,7},{7,1},{8,10},{10,12},{12... | collective-permute-start | bytes 786440 | tf_op jit(solution)/shard_map/ppermute | solution.py:52
  324.5 41.2 %collective-permute-start.52 = (bf16[544,1024]{1,0:T(8,128)(2,1)}, bf16[544,1024]{1,0:T(8,128)(2,1)}, u32[]{:S(2)}, u32[]{:S(2)}) collective-permute-start(bf16[544,1024]{1,0:T(8,128)(2,1)} %bitcast.57), channel_id=1, source_target_pairs={{0,1},{1,0},{2,3},{3,2},{4,5},{5,4},{6,7},{7,6},{8,9},{9,8},{10,11... | collective-permute-start | bytes 3342344 | tf_op jit(solution)/shard_map/ppermute | solution.py:28
  330.8 21.7 %all-to-all-start = ((f32[16,9,1024]{2,1,0:T(8,128)}), f32[16,9,1024]{2,1,0:T(8,128)S(1)}, u32[]{:S(2)}, u32[]{:S(2)}) async-start(f32[16,9,1024]{2,1,0:T(8,128)} %broadcast_in_dim.52), calls=%async_computation | async-start | bytes 2097152 | tf_op jit(solution)/shard_map/all_to_all | solution.py:68
  337.4 24.9 %collective-permute-start.63 = (bf16[272,1024]{1,0:T(8,128)(2,1)}, bf16[272,1024]{1,0:T(8,128)(2,1)}, u32[]{:S(2)}, u32[]{:S(2)}) collective-permute-start(bf16[272,1024]{1,0:T(8,128)(2,1)} %slice.656), channel_id=1, source_target_pairs={{0,24},{8,16},{16,8},{24,0},{1,25},{9,17},{17,9},{25,1},{2,26},{10... | collective-permute-start | bytes 1671176 | tf_op jit(solution)/shard_map/ppermute | solution.py:32
  347.5 52.9 %collective-permute-start.73 = (bf16[528,1024]{1,0:T(8,128)(2,1)}, bf16[528,1024]{1,0:T(8,128)(2,1)}, u32[]{:S(2)}, u32[]{:S(2)}) collective-permute-start(bf16[528,1024]{1,0:T(8,128)(2,1)} %slice.655), channel_id=1, source_target_pairs={{0,24},{8,16},{16,8},{24,0},{1,25},{9,17},{17,9},{25,1},{2,26},{10... | collective-permute-start | bytes 3244040 | tf_op jit(solution)/shard_map/ppermute | solution.py:32
  353.4 26.3 %all-to-all-start.1 = ((f32[8,9,1024]{2,1,0:T(8,128)}), f32[8,9,1024]{2,1,0:T(8,128)S(1)}, u32[]{:S(2)}, u32[]{:S(2)}) async-start(f32[8,9,1024]{2,1,0:T(8,128)} %broadcast_in_dim.53), calls=%async_computation.1 | async-start | bytes 1048576 | tf_op jit(solution)/shard_map/all_to_all | solution.py:68
  369.8 27.6 %collective-permute-start.53 = (bf16[272,1024]{1,0:T(8,128)(2,1)}, bf16[272,1024]{1,0:T(8,128)(2,1)}, u32[]{:S(2)}, u32[]{:S(2)}) collective-permute-start(bf16[272,1024]{1,0:T(8,128)(2,1)} %slice.657), channel_id=1, source_target_pairs={{0,24},{8,16},{16,8},{24,0},{1,25},{9,17},{17,9},{25,1},{2,26},{10... | collective-permute-start | bytes 1671176 | tf_op jit(solution)/shard_map/ppermute | solution.py:32
  402.8 18.0 %collective-permute-start.74 = (bf16[264,1024]{1,0:T(8,128)(2,1)S(1)}, bf16[264,1024]{1,0:T(8,128)(2,1)S(1)}, u32[]{:S(2)}, u32[]{:S(2)}) collective-permute-start(bf16[264,1024]{1,0:T(8,128)(2,1)S(1)} %dynamic-slice_convert_fusion), channel_id=1, source_target_pairs={{0,16},{16,0},{1,17},{17,1},{2,18},{18,2},{3,19},{19,3},{4,20},{20... | collective-permute-start | bytes 1622024 | tf_op jit(solution)/shard_map/ppermute | solution.py:36
  (202 other events, 1648.5 us)
